TPU v7x, 128 devices: a whole 4x4x4 slice. The times are simulated.
128 devices in a mesh: gy: 8 (over z_lo, x), gx: 16 (over z_hi, y, core).
Axes of the slice: x: 4, y: 4, z: 4 (z_hi: 2, z_lo: 2; z = z_hi * 2 + z_lo), core: 2. Of those that a mesh axis runs over, the one named last changes fastest.
Arguments:
- tracers: float32 [2, 8, 2048, 4096], P(None, None, 'gy', 'gx'), may hold values from -8 to 12, as said below
- face_speeds: float32 [2, 2, 8, 2048, 4096], P(None, None, None, 'gy', 'gx'), may hold values from -0.25 to 0.25, as said below
- ocean_block: int32 [256, 32], P('gy', 'gx'), may hold values from 0 to 1, as said below
- ice_blocks: int32 [8192], P(('gy', 'gx')), may hold values from -1 to 8191, as said below
Outputs:
- new_tracers: float32 [2, 8, 2048, 4096], P(None, None, 'gy', 'gx')
- density: float32 [8, 2048, 4096], P(None, 'gy', 'gx')
- ice_surface: float32 [8192, 3, 8, 128], P(('gy', 'gx'))
Inputs may be any that keep to these rules, and one draw needn't show every extreme that they name: `ocean_block`: 1 for an ocean block, 0 for land; at most half of the blocks of one device are land; some latitude block row has no land. `ice_blocks`: device d of the gy+gx order holds entries d * 64 to (d + 1) * 64 - 1, each the number of a block of its own latitude block row, or -1 for an empty slot. Every ocean block appears exactly once, no land block appears. At most 8 blocks of one device's grid go to one ice device, and this is reached in every draw; some ice device has all 64 slots filled in every draw. `tracers`: temperature anomalies lie within -8 to 12, salinity anomalies within -2 to 1.5. The top row's north faces are the fold: face_speeds[s, 1, k, 2047, i] = -face_speeds[s, 1, k, 2047, 4095 - i].
All inputs are finite; a program needn't handle non-finite values.
Results may differ from a plain program's by a relative error of at most 0.00002.
Values sent between devices are 32-bit elements; how exact they have to be, the bound alone decides.
A program may use at most 128 MiB of HBM per device.

v0:
```python
import jax
import jax.numpy as jnp
from jax import lax
from jax.sharding import PartitionSpec as P

BJ = 8
BI = 128


warming_swell_coefficient = 0.1655
haline_base = 0.7655
warming_swell_quadratic = 0.05952
haline_curve = 0.00054914
warming_compression_coupling = 0.0001497
haline_press = 1.109e-05
mixing_contraction_coefficient = 0.0024341
lateral_mix = 0.08
mixing_base = 0.05
mixing_boost = 0.2


def padded_2(value, sides, width, wrap):
    for axis, dim in sides:
        size, length = (lax.axis_size(axis), value.shape[dim])
        up = [(i, (i + 1) % size) for i in range(size if wrap else size - 1)]
        down = [(j, i) for i, j in up]
        last = lax.slice_in_dim(value, length - width, length, axis=dim)
        initial = lax.slice_in_dim(value, 0, width, axis=dim)
        before = lax.ppermute(last, axis, up)
        after = lax.ppermute(initial, axis, down)
        value = jnp.concatenate([before, value, after], axis=dim)
    return value


def seawater_mass_per_volume(heat_grid_values, saltiness_grid_values, depth_layer_count):
    return (
        -warming_swell_coefficient
        * (
            1.0
            + 0.5 * warming_swell_quadratic * heat_grid_values
            + warming_compression_coupling * depth_layer_count
        )
        * heat_grid_values
        + haline_base
        * (1.0 - 0.5 * haline_curve * saltiness_grid_values - haline_press * depth_layer_count)
        * saltiness_grid_values
        - mixing_contraction_coefficient * heat_grid_values * saltiness_grid_values
    )


def face_flux(velocity, lower_cells, upper_cells):
    return (
        jnp.maximum(velocity, 0.0) * lower_cells
        + jnp.minimum(velocity, 0.0) * upper_cells
        - lateral_mix * (upper_cells - lower_cells)
    )


def mirror_row(edge_rows):
    column_count = lax.axis_size("gx")
    tracer_count, levels, row_width = edge_rows.shape
    piece_width = row_width // column_count
    split_rows = edge_rows.reshape(tracer_count, levels, column_count, piece_width)
    spread = lax.all_to_all(split_rows, "gx", split_axis=2, concat_axis=2, tiled=True)
    returned = lax.all_to_all(spread[:, :, ::-1, :], "gx", split_axis=2, concat_axis=2, tiled=True)
    return returned.reshape(tracer_count, levels, row_width)[..., ::-1]


def advance(fields, velocity, ocean_mask, at_top, south_open):
    east_ext = padded_2(jnp.concatenate([fields, velocity[0:1]], axis=0), (("gx", 3),), 1, True)
    cell_values = east_ext[0:2]
    east_all = face_flux(east_ext[2][:, :, :-1], cell_values[..., :-1], cell_values[..., 1:])
    north_ext = padded_2(jnp.concatenate([fields, velocity[1:2]], axis=0), (("gy", 2),), 1, False)
    mirrored = mirror_row(fields[:, :, -1, :])
    north_edge = jnp.where(at_top, mirrored[:, :, None, :], north_ext[0:2, :, -1:, :])
    upper_cells = jnp.concatenate([north_ext[0:2, :, 1:-1], north_edge], axis=2)
    north_all = face_flux(north_ext[2][:, :-1], north_ext[0:2, :, :-1], upper_cells)
    keep_face = jnp.where(jnp.arange(north_all.shape[2]) == 0, south_open, 1.0)[:, None]
    north_all = north_all * keep_face
    change = east_all[..., 1:] - east_all[..., :-1] + (north_all[:, :, 1:] - north_all[:, :, :-1])
    return fields - ocean_mask * change


def vertical(fields, density, ocean_mask):
    diffusivity = mixing_base + mixing_boost * jax.nn.sigmoid(-2.0 * (density[1:] - density[:-1]))
    vertical_flux = diffusivity * (fields[:, 1:] - fields[:, :-1])
    zero_layer = jnp.zeros_like(fields[:, :1])
    padded = jnp.concatenate([zero_layer, vertical_flux, zero_layer], axis=1)
    return fields + ocean_mask * (padded[:, 1:] - padded[:, :-1])


def relay_surface(surface, ice_blocks, row_index, column_index):
    field_count, block_rows, block_cols = surface.shape
    rows_device = block_rows // BJ
    cols_device = block_cols // BI
    per_device = rows_device * cols_device
    column_count = lax.axis_size("gx")
    capacity = per_device // 8
    all_cols = cols_device * column_count
    ice_count = ice_blocks.shape[0]
    tile_stack = surface.reshape(field_count, rows_device, BJ, cols_device, BI).transpose(
        1, 3, 0, 2, 4
    )
    tile_stack = tile_stack.reshape(per_device, field_count, BJ, BI)
    listing = lax.all_gather(ice_blocks, "gx", axis=0, tiled=True)
    local_ids = jnp.arange(per_device, dtype=jnp.int32)
    tile_ids = (
        (row_index * rows_device + local_ids // cols_device) * all_cols
        + column_index * cols_device
        + local_ids % cols_device
    )
    matches = listing[None, :] == tile_ids[:, None]
    has_owner = jnp.any(matches, axis=1)
    target = jnp.argmax(matches, axis=1) // ice_count
    earlier = (
        (target[None, :] == target[:, None])
        & has_owner[None, :]
        & (local_ids[None, :] < local_ids[:, None])
    )
    rank_here = jnp.sum(earlier.astype(jnp.int32), axis=1)
    position = jnp.where(has_owner, target * capacity + rank_here, column_count * capacity)
    outgoing = (
        jnp.zeros((column_count * capacity, field_count, BJ, BI), jnp.float32)
        .at[position]
        .set(tile_stack, mode="drop")
    )
    incoming = lax.all_to_all(outgoing, "gx", split_axis=0, concat_axis=0, tiled=True)
    filled = ice_blocks >= 0
    block_ids = jnp.maximum(ice_blocks, 0)
    source = block_ids % all_cols // cols_device
    local_tile = (
        block_ids // all_cols - row_index * rows_device
    ) * cols_device + block_ids % cols_device
    before = (
        (source[None, :] == source[:, None])
        & filled[None, :]
        & (local_tile[None, :] < local_tile[:, None])
    )
    rank_there = jnp.sum(before.astype(jnp.int32), axis=1)
    picked = incoming[source * capacity + rank_there]
    return jnp.where(filled[:, None, None, None], picked, 0.0)


def on_device(tracers, face_speeds, ocean_block, ice_blocks):
    row_index = lax.axis_index("gy")
    column_index = lax.axis_index("gx")
    at_top = row_index == lax.axis_size("gy") - 1
    south_open = (row_index > 0).astype(jnp.float32)
    ocean_mask = jnp.repeat(jnp.repeat(ocean_block.astype(jnp.float32), BJ, 0), BI, 1)
    levels = tracers.shape[1]
    depth_layer_count = (10.0 * jnp.arange(levels, dtype=jnp.float32) + 5.0)[:, None, None]
    fields = tracers
    for step_index in range(face_speeds.shape[0]):
        fields = advance(fields, face_speeds[step_index], ocean_mask, at_top, south_open)
        fields = vertical(
            fields, seawater_mass_per_volume(fields[0], fields[1], depth_layer_count), ocean_mask
        )
    density = seawater_mass_per_volume(fields[0], fields[1], depth_layer_count)
    surface = jnp.stack([fields[0, 0], fields[1, 0], density[0]])
    relayed = relay_surface(surface, ice_blocks, row_index, column_index)
    return (fields, density, relayed)


def solution(mesh):
    return jax.shard_map(
        on_device,
        mesh=mesh,
        in_specs=(
            P(None, None, "gy", "gx"),
            P(None, None, None, "gy", "gx"),
            P("gy", "gx"),
            P(("gy", "gx")),
        ),
        out_specs=(
            P(None, None, "gy", "gx"),
            P(None, "gy", "gx"),
            P(("gy", "gx"), None, None, None),
        ),
        check_vma=False,
    )
```

profile of v0, /device:TPU:32, one launch (start us, length us, event | category | flops | bytes accessed | tf_op | source)
XLA Modules:
  0.0 244.4 jit_solution(15026861289584952493)
XLA Ops:
  0.6 5.4 %copy.146 = f32[2,8,256,256]{2,1,3,0:T(8,128)} copy(f32[2,8,256,256]{3,2,1,0:T(8,128)} %param.4) | data formatting | bytes 8388608 | tf_op args[0]
  6.1 7.0 %fusion.39 = (f32[1,1,8,256,256]{4,3,2,1,0:T(8,128)}, f32[1,1,8,256,256]{4,3,2,1,0:T(8,128)}, f32[1,1,8,256,256]{4,3,2,1,0:T(8,128)}, f32[1,1,8,256,256]{4,3,2,1,0:T(8,128)}) fusion(f32[2,2,8,256,256]{4,3,2,1,0:T(8,128)} %param.5), kind=kLoop, calls=%fused_computation.142 | loop fusion | bytes 16777216 | tf_op jit(solution)/shard_map/slice | solution.py:70
  13.0 2.2 copy.166
  15.3 6.5 %fusion.9 = (f32[3,8,1,256]{2,1,3,0:T(8,128)}, f32[3,8,1,256]{2,1,3,0:T(8,128)}) fusion(f32[1,8,256,256]{2,1,3,0:T(8,128)S(1)} %bitcast.77, f32[2,8,256,256]{2,1,3,0:T(8,128)} %copy.146), kind=kLoop, calls=%fused_computation.45 | loop fusion | flops 12288 | bytes 6340608 | tf_op jit(solution)/shard_map/concatenate | solution.py:73
  21.8 2.5 %copy.136 = f32[3,8,1,256]{3,1,2,0:T(8,128)S(1)} copy(f32[3,8,1,256]{2,1,3,0:T(8,128)} %get-tuple-element.30) | data formatting | bytes 49152 | tf_op jit(solution)/shard_map/slice | solution.py:27
  24.3 3.4 %collective-permute-start.2 = (f32[3,8,1,256]{3,1,2,0:T(8,128)S(1)}, f32[3,8,1,256]{3,1,2,0:T(8,128)S(1)}, u32[]{:S(2)}, u32[]{:S(2)}) collective-permute-start(f32[3,8,1,256]{3,1,2,0:T(8,128)S(1)} %copy.136), channel_id=1, source_target_pairs={{0,16},{16,32},{32,48},{48,64},{64,80},{80,96},{96,112},{1,17},{17... | collective-permute-start | bytes 73736 | tf_op jit(solution)/shard_map/ppermute | solution.py:29
  28.9 4.6 %collective-permute-start.3 = (f32[3,8,1,256]{3,1,2,0:T(8,128)S(1)}, f32[3,8,1,256]{3,1,2,0:T(8,128)S(1)}, u32[]{:S(2)}, u32[]{:S(2)}) collective-permute-start(f32[3,8,1,256]{3,1,2,0:T(8,128)S(1)} %copy.137), channel_id=1, source_target_pairs={{16,0},{32,16},{48,32},{64,48},{80,64},{96,80},{112,96},{17,1},{33... | collective-permute-start | bytes 73736 | tf_op jit(solution)/shard_map/ppermute | solution.py:30
  35.3 7.0 %all-to-all-start = ((f32[16,1,256]{2,1,0:T(1,128)}), f32[16,1,256]{2,1,0:T(1,128)S(1)}, u32[]{:S(2)}, u32[]{:S(2)}) async-start(f32[16,1,256]{2,1,0:T(1,128)} %reshape.117), calls=%async_computation | async-start | bytes 32768 | tf_op jit(solution)/shard_map/all_to_all | solution.py:64
  42.3 2.2 copy.165
  46.2 5.0 %collective-permute-start.1 = (f32[3,8,256,1]{2,1,3,0:T(8,128)S(1)}, f32[3,8,256,1]{2,1,3,0:T(8,128)S(1)}, u32[]{:S(2)}, u32[]{:S(2)}) collective-permute-start(f32[3,8,256,1]{2,1,3,0:T(8,128)S(1)} %get-tuple-element.29), channel_id=1, source_target_pairs={{1,0},{2,1},{3,2},{4,3},{5,4},{6,5},{7,6},{8,7},{9,8},{10,9},{11,1... | collective-permute-start | bytes 73736 | tf_op jit(solution)/shard_map/ppermute | solution.py:30
  52.8 10.8 %all-reduce.4 = s32[1024]{0:T(1024)S(1)} all-reduce(s32[1024]{0:T(1024)S(1)} %dynamic-update-slice), channel_id=1, replica_groups=mesh['gy'=8,'gx'=16] {'gx'}, use_global_device_ids=true, to_apply=%add.4 | all-reduce | flops 1024 | bytes 8192
  65.1 3.1 %copy.167 = f32[1,1,8,256,256]{3,2,4,1,0:T(8,128)} copy(f32[1,1,8,256,256]{4,3,2,1,0:T(8,128)} %get-tuple-element.20) | data formatting | bytes 4194304
  68.1 2.2 copy.168
  72.5 5.3 %all-to-all-start.1 = ((f32[16,1,256]{2,1,0:T(1,128)}), f32[16,1,256]{2,1,0:T(1,128)S(1)}, u32[]{:S(2)}, u32[]{:S(2)}) async-start(f32[16,1,256]{2,1,0:T(1,128)} %reshape.119), calls=%async_computation.1 | async-start | bytes 32768 | tf_op jit(solution)/shard_map/all_to_all | solution.py:65
  79.6 2.3 slice_maximum_fusion.3
  81.9 2.2 copy.138
  84.1 2.2 copy.139
  86.3 3.5 %fusion.11 = f32[8,258,256]{1,0,2:T(8,128)S(1)} fusion(f32[3,8,1,256]{2,1,3,0:T(8,128)} %copy.139, f32[3,8,1,256]{2,1,3,0:T(8,128)} %copy.138, f32[1,8,256,256]{2,1,3,0:T(8,128)} %bitcast.78, f32[2,8,256,256]{2,1,3,0:T(8,128)} %copy.146), kind=kLoop, calls=%fused_computation.52 | loop fusion | flops 1585152 | bytes 8454144 | tf_op jit(solution)/shard_map/squeeze | solution.py:77
  91.6 2.6 %multiply_subtract_fusion.1 = f32[2,8,256,257]{2,1,3,0:T(8,128)} fusion(f32[3,8,256,1]{2,1,3,0:T(8,128)S(1)} %collective-permute-done.1, f32[1,8,256,256]{2,1,3,0:T(8,128)S(1)} %bitcast.85, f32[2,8,256,256]{2,1,3,0:T(8,128)S(1)} %copy-done.3, f32[3,8,256,1]{2,1,3,0:T(8,128)S(1)} %collective-permute-done, f32[8,256,257]{1,0,2:T(8,128)S(1)} %copy-done.14, ...), kind=kLoop, calls=%fused_computation.27 | loop fusion | flops 10526720 | bytes 14761984 | tf_op jit(solution)/shard_map/sub | solution.py:53
  94.2 3.1 %slice_maximum_fusion.1 = (f32[8,257,256]{1,0,2:T(8,128)}, f32[8,257,256]{1,0,2:T(8,128)}) fusion(f32[8,258,256]{1,0,2:T(8,128)S(1)} %fusion.11), kind=kLoop, calls=%fused_computation.59 | loop fusion | flops 1052672 | bytes 6316032 | tf_op jit(solution)/shard_map/max | solution.py:53
  97.3 1.9 copy.144
  100.5 2.0 copy.143
  102.4 1.9 broadcast_select_fusion.1
  105.9 5.8 %subtract_multiply_fusion.1 = f32[2,8,257,256]{2,1,3,0:T(8,128)S(1)} fusion(f32[2,8,1,256]{2,1,3,0:T(8,128)S(1)} %broadcast_select_fusion.1, f32[2,8,256,256]{2,1,3,0:T(8,128)S(1)} %copy-done.4, f32[1,8,256,256]{2,1,3,0:T(8,128)S(1)} %bitcast.79, f32[3,8,1,256]{2,1,3,0:T(8,128)} %copy.138, f32[257]{0:T(512)S(1)} %fusion.31, ...), kind=kLoop, calls=%fused_computation.15 | loop fusion | flops 10526720 | bytes 14754820 | tf_op jit(solution)/shard_map/mul | solution.py:79
  116.7 1.9 slice.289
  120.3 5.0 %collective-permute-start.5 = (f32[3,8,256,1]{2,1,3,0:T(8,128)S(1)}, f32[3,8,256,1]{2,1,3,0:T(8,128)S(1)}, u32[]{:S(2)}, u32[]{:S(2)}) collective-permute-start(f32[3,8,256,1]{2,1,3,0:T(8,128)S(1)} %get-tuple-element.25), channel_id=1, source_target_pairs={{1,0},{2,1},{3,2},{4,3},{5,4},{6,5},{7,6},{8,7},{9,8},{10,9},{11,1... | collective-permute-start | bytes 73736 | tf_op jit(solution)/shard_map/ppermute | solution.py:30
  125.2 2.2 copy.154
  128.3 4.8 %all-to-all-start.2 = ((f32[16,1,256]{2,1,0:T(1,128)}), f32[16,1,256]{2,1,0:T(1,128)S(1)}, u32[]{:S(2)}, u32[]{:S(2)}) async-start(f32[16,1,256]{2,1,0:T(1,128)} %reshape.121), calls=%async_computation.2 | async-start | bytes 32768 | tf_op jit(solution)/shard_map/all_to_all | solution.py:64
  133.1 5.8 %fusion.8 = (f32[3,8,1,256]{2,1,3,0:T(8,128)}, f32[3,8,1,256]{2,1,3,0:T(8,128)}) fusion(f32[1,8,256,256]{2,1,3,0:T(8,128)S(1)} %bitcast.74, f32[2,8,256,256]{2,1,3,0:T(8,128)} %copy-done), kind=kLoop, calls=%fused_computation.44 | loop fusion | flops 12288 | bytes 6340608 | tf_op jit(solution)/shard_map/concatenate | solution.py:73
  138.9 2.4 copy.149
  143.2 2.4 copy.150
  145.6 6.0 %collective-permute-start.7 = (f32[3,8,1,256]{3,1,2,0:T(8,128)S(1)}, f32[3,8,1,256]{3,1,2,0:T(8,128)S(1)}, u32[]{:S(2)}, u32[]{:S(2)}) collective-permute-start(f32[3,8,1,256]{3,1,2,0:T(8,128)S(1)} %copy.150), channel_id=1, source_target_pairs={{16,0},{32,16},{48,32},{64,48},{80,64},{96,80},{112,96},{17,1},{33... | collective-permute-start | bytes 73736 | tf_op jit(solution)/shard_map/ppermute | solution.py:30
  153.2 7.2 %all-to-all-start.3 = ((f32[16,1,256]{2,1,0:T(1,128)}), f32[16,1,256]{2,1,0:T(1,128)S(1)}, u32[]{:S(2)}, u32[]{:S(2)}) async-start(f32[16,1,256]{2,1,0:T(1,128)} %reshape.123), calls=%async_computation.3 | async-start | bytes 32768 | tf_op jit(solution)/shard_map/all_to_all | solution.py:65
  162.2 2.3 slice_maximum_fusion.2
  164.5 2.2 copy.151
  166.7 2.2 copy.152
  168.9 2.8 %fusion.10 = f32[8,258,256]{1,0,2:T(8,128)S(1)} fusion(f32[3,8,1,256]{2,1,3,0:T(8,128)} %copy.152, f32[3,8,1,256]{2,1,3,0:T(8,128)} %copy.151, f32[1,8,256,256]{2,1,3,0:T(8,128)S(1)} %bitcast.75, f32[2,8,256,256]{2,1,3,0:T(8,128)} %copy-done), kind=kLoop, calls=%fused_computation.47 | loop fusion | flops 1585152 | bytes 8454144 | tf_op jit(solution)/shard_map/squeeze | solution.py:77
  173.6 2.6 %multiply_subtract_fusion = f32[2,8,256,257]{2,1,3,0:T(8,128)} fusion(f32[3,8,256,1]{2,1,3,0:T(8,128)S(1)} %collective-permute-done.5, f32[1,8,256,256]{2,1,3,0:T(8,128)S(1)} %bitcast.82, f32[2,8,256,256]{2,1,3,0:T(8,128)S(1)} %copy-done.1, f32[3,8,256,1]{2,1,3,0:T(8,128)S(1)} %collective-permute-done.4, f32[8,256,257]{1,0,2:T(8,128)S(1)} %copy-done.16, ...), kind=kLoop, calls=%fused_computation.26 | loop fusion | flops 10526720 | bytes 14761984 | tf_op jit(solution)/shard_map/sub | solution.py:53
  176.2 3.1 %slice_maximum_fusion = (f32[8,257,256]{1,0,2:T(8,128)}, f32[8,257,256]{1,0,2:T(8,128)}) fusion(f32[8,258,256]{1,0,2:T(8,128)S(1)} %fusion.10), kind=kLoop, calls=%fused_computation.57 | loop fusion | flops 1052672 | bytes 6316032 | tf_op jit(solution)/shard_map/max | solution.py:53
  179.3 2.0 copy.158
  182.4 2.0 copy.157
  184.4 1.9 broadcast_select_fusion
  187.2 5.9 %subtract_multiply_fusion = f32[2,8,257,256]{2,1,3,0:T(8,128)S(1)} fusion(f32[2,8,1,256]{2,1,3,0:T(8,128)S(1)} %broadcast_select_fusion, f32[2,8,256,256]{2,1,3,0:T(8,128)S(1)} %copy-done.2, f32[1,8,256,256]{2,1,3,0:T(8,128)S(1)} %bitcast.76, f32[3,8,1,256]{2,1,3,0:T(8,128)} %copy.151, f32[8,257,256]{1,0,2:T(8,128)} %get-tuple-element.35, ...), kind=kLoop, calls=%fused_computation.14 | loop fusion | flops 10526720 | bytes 14754820 | tf_op jit(solution)/shard_map/mul | solution.py:79
  202.3 8.1 %scatter_fusion = f32[128,3,8,128]{3,2,1,0:T(8,128)} fusion(f32[128,3,8,128]{3,2,1,0:T(8,128)} %broadcast_in_dim.78, s32[64]{0:T(128)S(1)} %compare_select_fusion.1, f32[64,3,8,128]{3,2,1,0:T(8,128)S(1)} %copy.162), kind=kCustom, calls=%fused_computation.1 | custom fusion | bytes 2359552 | tf_op jit(solution)/shard_map/scatter | solution.py:125
  210.3 7.4 %all-to-all-start.4 = ((f32[128,3,8,128]{3,2,1,0:T(8,128)}), f32[128,3,8,128]{3,2,1,0:T(8,128)}, u32[]{:S(2)}, u32[]{:S(2)}) async-start(f32[128,3,8,128]{3,2,1,0:T(8,128)} %scatter_fusion), calls=%async_computation.4 | async-start | bytes 3145728 | tf_op jit(solution)/shard_map/all_to_all | solution.py:127
  219.8 5.2 %copy.163 = f32[2,8,256,256]{3,2,1,0:T(8,128)} copy(f32[2,8,256,256]{2,1,3,0:T(8,128)} %copy-done.5) | data formatting | bytes 8388608
  225.0 16.4 %all-to-all-done.4 = f32[128,3,8,128]{3,2,1,0:T(8,128)} async-done(((f32[128,3,8,128]{3,2,1,0:T(8,128)}), f32[128,3,8,128]{3,2,1,0:T(8,128)}, u32[]{:S(2)}, u32[]{:S(2)}) %all-to-all-start.4) | async-done | bytes 1572896 | tf_op jit(solution)/shard_map/all_to_all | solution.py:127
  241.4 2.0 gather_fusion
  (138 shorter events, 43.8 us)
Async XLA Ops:
  15.3 6.6 %copy-start.6 = (f32[1,1,8,256,256]{3,2,4,1,0:T(8,128)}, f32[1,1,8,256,256]{3,2,4,1,0:T(8,128)S(1)}, u32[]{:S(2)}) copy-start(f32[1,1,8,256,256]{3,2,4,1,0:T(8,128)S(1)} %copy.166) | copy-start | bytes 6291460
  21.8 5.9 %copy-start.12 = (f32[3,8,1,256]{2,1,3,0:T(8,128)S(1)}, f32[3,8,1,256]{2,1,3,0:T(8,128)}, u32[]{:S(2)}) copy-start(f32[3,8,1,256]{2,1,3,0:T(8,128)} %get-tuple-element.31) | copy-start | bytes 73732
  24.3 57.6 %collective-permute-start.2 = (f32[3,8,1,256]{3,1,2,0:T(8,128)S(1)}, f32[3,8,1,256]{3,1,2,0:T(8,128)S(1)}, u32[]{:S(2)}, u32[]{:S(2)}) collective-permute-start(f32[3,8,1,256]{3,1,2,0:T(8,128)S(1)} %copy.136), channel_id=1, source_target_pairs={{0,16},{16,32},{32,48},{48,64},{64,80},{80,96},{96,112},{1,17},{17... | collective-permute-start | bytes 73736 | tf_op jit(solution)/shard_map/ppermute | solution.py:29
  28.9 55.2 %collective-permute-start.3 = (f32[3,8,1,256]{3,1,2,0:T(8,128)S(1)}, f32[3,8,1,256]{3,1,2,0:T(8,128)S(1)}, u32[]{:S(2)}, u32[]{:S(2)}) collective-permute-start(f32[3,8,1,256]{3,1,2,0:T(8,128)S(1)} %copy.137), channel_id=1, source_target_pairs={{16,0},{32,16},{48,32},{64,48},{80,64},{96,80},{112,96},{17,1},{33... | collective-permute-start | bytes 73736 | tf_op jit(solution)/shard_map/ppermute | solution.py:30
  35.3 35.0 %all-to-all-start = ((f32[16,1,256]{2,1,0:T(1,128)}), f32[16,1,256]{2,1,0:T(1,128)S(1)}, u32[]{:S(2)}, u32[]{:S(2)}) async-start(f32[16,1,256]{2,1,0:T(1,128)} %reshape.117), calls=%async_computation | async-start | bytes 32768 | tf_op jit(solution)/shard_map/all_to_all | solution.py:64
  44.5 1.3 copy-start.10
  44.6 6.6 %copy-start.19 = (u32[128]{0:T(128)S(1)}, u32[128]{0:T(128)}, u32[]{:S(2)}) copy-start(u32[128]{0:T(128)} %constant.152) | copy-start | bytes 1540
  44.6 8.0 %copy-start.18 = (s32[64]{0:T(128)S(1)}, s32[64]{0:T(128)}, u32[]{:S(2)}) copy-start(s32[64]{0:T(128)} %param.7) | copy-start | bytes 772
  44.6 20.3 %copy-start.17 = (s32[32,2]{0,1:T(2,128)S(1)}, s32[32,2]{0,1:T(2,128)}, u32[]{:S(2)}) copy-start(s32[32,2]{0,1:T(2,128)} %param.6) | copy-start | bytes 772
  45.8 32.0 %collective-permute-start = (f32[3,8,256,1]{2,1,3,0:T(8,128)S(1)}, f32[3,8,256,1]{2,1,3,0:T(8,128)S(1)}, u32[]{:S(2)}, u32[]{:S(2)}) collective-permute-start(f32[3,8,256,1]{2,1,3,0:T(8,128)S(1)} %get-tuple-element.28), channel_id=1, source_target_pairs={{0,1},{1,2},{2,3},{3,4},{4,5},{5,6},{6,7},{7,8},{8,9},{9,10},{10,1... | collective-permute-start | bytes 73736 | tf_op jit(solution)/shard_map/ppermute | solution.py:29
  46.2 31.6 %collective-permute-start.1 = (f32[3,8,256,1]{2,1,3,0:T(8,128)S(1)}, f32[3,8,256,1]{2,1,3,0:T(8,128)S(1)}, u32[]{:S(2)}, u32[]{:S(2)}) collective-permute-start(f32[3,8,256,1]{2,1,3,0:T(8,128)S(1)} %get-tuple-element.29), channel_id=1, source_target_pairs={{1,0},{2,1},{3,2},{4,3},{5,4},{6,5},{7,6},{8,7},{9,8},{10,9},{11,1... | collective-permute-start | bytes 73736 | tf_op jit(solution)/shard_map/ppermute | solution.py:30
  72.5 26.8 %all-to-all-start.1 = ((f32[16,1,256]{2,1,0:T(1,128)}), f32[16,1,256]{2,1,0:T(1,128)S(1)}, u32[]{:S(2)}, u32[]{:S(2)}) async-start(f32[16,1,256]{2,1,0:T(1,128)} %reshape.119), calls=%async_computation.1 | async-start | bytes 32768 | tf_op jit(solution)/shard_map/all_to_all | solution.py:65
  86.3 3.5 %copy-start.3 = (f32[2,8,256,256]{2,1,3,0:T(8,128)S(1)}, f32[2,8,256,256]{2,1,3,0:T(8,128)}, u32[]{:S(2)}) copy-start(f32[2,8,256,256]{2,1,3,0:T(8,128)} %copy.146) | copy-start | bytes 12582916
  86.3 4.1 %copy-start.11 = (f32[1,1,8,256,256]{3,2,4,1,0:T(8,128)S(1)}, f32[1,1,8,256,256]{3,2,4,1,0:T(8,128)}, u32[]{:S(2)}) copy-start(f32[1,1,8,256,256]{3,2,4,1,0:T(8,128)} %copy-done.10) | copy-start | bytes 6291460
  86.3 4.7 %copy-start.13 = (f32[8,256,257]{1,0,2:T(8,128)S(1)}, f32[8,256,257]{1,0,2:T(8,128)}, u32[]{:S(2)}) copy-start(f32[8,256,257]{1,0,2:T(8,128)} %get-tuple-element.40) | copy-start | bytes 6316036
  86.3 5.3 %copy-start.14 = (f32[8,256,257]{1,0,2:T(8,128)S(1)}, f32[8,256,257]{1,0,2:T(8,128)}, u32[]{:S(2)}) copy-start(f32[8,256,257]{1,0,2:T(8,128)} %get-tuple-element.41) | copy-start | bytes 6316036
  102.4 2.8 %copy-start.4 = (f32[2,8,256,256]{2,1,3,0:T(8,128)S(1)}, f32[2,8,256,256]{2,1,3,0:T(8,128)}, u32[]{:S(2)}) copy-start(f32[2,8,256,256]{2,1,3,0:T(8,128)} %copy.146) | copy-start | bytes 12582916
  102.4 3.5 %copy-start.7 = (f32[1,1,8,256,256]{3,2,4,1,0:T(8,128)S(1)}, f32[1,1,8,256,256]{3,2,4,1,0:T(8,128)}, u32[]{:S(2)}) copy-start(f32[1,1,8,256,256]{3,2,4,1,0:T(8,128)} %copy-done.6) | copy-start | bytes 6291460
  104.4 7.4 %slice-start.2 = ((s8[4210688]{0:T(1024)(128)(4,1)}), s8[4194304]{0:T(1024)(128)(4,1)S(1)}, s32[]{:S(2)}) async-start(s8[4210688]{0:T(1024)(128)(4,1)} %bitcast.72), calls=%async_computation.7 | async-start | bytes 8388608
  105.9 5.9 %slice-start.3 = ((s8[4210688]{0:T(1024)(128)(4,1)}), s8[16384]{0:T(1024)(128)(4,1)S(1)}, s32[]{:S(2)}) async-start(s8[4210688]{0:T(1024)(128)(4,1)} %bitcast.72), calls=%async_computation.8 | async-start | bytes 32768
  116.7 3.1 %copy-start = (f32[2,8,256,256]{2,1,3,0:T(8,128)}, f32[2,8,256,256]{2,1,3,0:T(8,128)S(1)}, u32[]{:S(2)}) copy-start(f32[2,8,256,256]{2,1,3,0:T(8,128)S(1)} %multiply_add_fusion.1) | copy-start | bytes 12582916
  116.7 3.1 %copy-start.8 = (f32[1,1,8,256,256]{3,2,4,1,0:T(8,128)S(1)}, f32[1,1,8,256,256]{3,2,4,1,0:T(8,128)}, u32[]{:S(2)}) copy-start(f32[1,1,8,256,256]{3,2,4,1,0:T(8,128)} %copy.167) | copy-start | bytes 6291460
  119.9 40.6 %collective-permute-start.4 = (f32[3,8,256,1]{2,1,3,0:T(8,128)S(1)}, f32[3,8,256,1]{2,1,3,0:T(8,128)S(1)}, u32[]{:S(2)}, u32[]{:S(2)}) collective-permute-start(f32[3,8,256,1]{2,1,3,0:T(8,128)S(1)} %get-tuple-element.24), channel_id=1, source_target_pairs={{0,1},{1,2},{2,3},{3,4},{4,5},{5,6},{6,7},{7,8},{8,9},{9,10},{10,1... | collective-permute-start | bytes 73736 | tf_op jit(solution)/shard_map/ppermute | solution.py:29
  120.3 40.2 %collective-permute-start.5 = (f32[3,8,256,1]{2,1,3,0:T(8,128)S(1)}, f32[3,8,256,1]{2,1,3,0:T(8,128)S(1)}, u32[]{:S(2)}, u32[]{:S(2)}) collective-permute-start(f32[3,8,256,1]{2,1,3,0:T(8,128)S(1)} %get-tuple-element.25), channel_id=1, source_target_pairs={{1,0},{2,1},{3,2},{4,3},{5,4},{6,5},{7,6},{8,7},{9,8},{10,9},{11,1... | collective-permute-start | bytes 73736 | tf_op jit(solution)/shard_map/ppermute | solution.py:30
  128.3 23.3 %all-to-all-start.2 = ((f32[16,1,256]{2,1,0:T(1,128)}), f32[16,1,256]{2,1,0:T(1,128)S(1)}, u32[]{:S(2)}, u32[]{:S(2)}) async-start(f32[16,1,256]{2,1,0:T(1,128)} %reshape.121), calls=%async_computation.2 | async-start | bytes 32768 | tf_op jit(solution)/shard_map/all_to_all | solution.py:64
  141.3 23.2 %collective-permute-start.6 = (f32[3,8,1,256]{3,1,2,0:T(8,128)S(1)}, f32[3,8,1,256]{3,1,2,0:T(8,128)S(1)}, u32[]{:S(2)}, u32[]{:S(2)}) collective-permute-start(f32[3,8,1,256]{3,1,2,0:T(8,128)S(1)} %copy.149), channel_id=1, source_target_pairs={{0,16},{16,32},{32,48},{48,64},{64,80},{80,96},{96,112},{1,17},{17... | collective-permute-start | bytes 73736 | tf_op jit(solution)/shard_map/ppermute | solution.py:29
  145.6 21.1 %collective-permute-start.7 = (f32[3,8,1,256]{3,1,2,0:T(8,128)S(1)}, f32[3,8,1,256]{3,1,2,0:T(8,128)S(1)}, u32[]{:S(2)}, u32[]{:S(2)}) collective-permute-start(f32[3,8,1,256]{3,1,2,0:T(8,128)S(1)} %copy.150), channel_id=1, source_target_pairs={{16,0},{32,16},{48,32},{64,48},{80,64},{96,80},{112,96},{17,1},{33... | collective-permute-start | bytes 73736 | tf_op jit(solution)/shard_map/ppermute | solution.py:30
  153.2 28.1 %all-to-all-start.3 = ((f32[16,1,256]{2,1,0:T(1,128)}), f32[16,1,256]{2,1,0:T(1,128)S(1)}, u32[]{:S(2)}, u32[]{:S(2)}) async-start(f32[16,1,256]{2,1,0:T(1,128)} %reshape.123), calls=%async_computation.3 | async-start | bytes 32768 | tf_op jit(solution)/shard_map/all_to_all | solution.py:65
  168.9 2.9 %copy-start.1 = (f32[2,8,256,256]{2,1,3,0:T(8,128)S(1)}, f32[2,8,256,256]{2,1,3,0:T(8,128)}, u32[]{:S(2)}) copy-start(f32[2,8,256,256]{2,1,3,0:T(8,128)} %copy-done) | copy-start | bytes 12582916
  168.9 3.5 %copy-start.9 = (f32[1,1,8,256,256]{3,2,4,1,0:T(8,128)S(1)}, f32[1,1,8,256,256]{3,2,4,1,0:T(8,128)}, u32[]{:S(2)}) copy-start(f32[1,1,8,256,256]{3,2,4,1,0:T(8,128)} %copy.167) | copy-start | bytes 6291460
  168.9 4.1 %copy-start.15 = (f32[8,256,257]{1,0,2:T(8,128)S(1)}, f32[8,256,257]{1,0,2:T(8,128)}, u32[]{:S(2)}) copy-start(f32[8,256,257]{1,0,2:T(8,128)} %get-tuple-element.38) | copy-start | bytes 6316036
  168.9 4.7 %copy-start.16 = (f32[8,256,257]{1,0,2:T(8,128)S(1)}, f32[8,256,257]{1,0,2:T(8,128)}, u32[]{:S(2)}) copy-start(f32[8,256,257]{1,0,2:T(8,128)} %get-tuple-element.39) | copy-start | bytes 6316036
  184.4 2.8 %copy-start.2 = (f32[2,8,256,256]{2,1,3,0:T(8,128)S(1)}, f32[2,8,256,256]{2,1,3,0:T(8,128)}, u32[]{:S(2)}) copy-start(f32[2,8,256,256]{2,1,3,0:T(8,128)} %copy-done) | copy-start | bytes 12582916
  184.4 8.7 %slice-start = ((s8[4210688]{0:T(1024)(128)(4,1)}), s8[4194304]{0:T(1024)(128)(4,1)S(1)}, s32[]{:S(2)}) async-start(s8[4210688]{0:T(1024)(128)(4,1)} %bitcast.70), calls=%async_computation.5 | async-start | bytes 8388608
  187.2 5.9 %slice-start.1 = ((s8[4210688]{0:T(1024)(128)(4,1)}), s8[16384]{0:T(1024)(128)(4,1)S(1)}, s32[]{:S(2)}) async-start(s8[4210688]{0:T(1024)(128)(4,1)} %bitcast.70), calls=%async_computation.6 | async-start | bytes 32768
  198.1 2.0 copy-start.5
  210.3 31.0 %all-to-all-start.4 = ((f32[128,3,8,128]{3,2,1,0:T(8,128)}), f32[128,3,8,128]{3,2,1,0:T(8,128)}, u32[]{:S(2)}, u32[]{:S(2)}) async-start(f32[128,3,8,128]{3,2,1,0:T(8,128)} %scatter_fusion), calls=%async_computation.4 | async-start | bytes 3145728 | tf_op jit(solution)/shard_map/all_to_all | solution.py:127
where the time goes:
time: 246 us; the launch traced here: 244 us
  local copies, waits for them, and re-layouts  85.9 us (35%)
  other arithmetic  70.9 us (29%)
  starting transfers between devices  58.3 us (24%)
  waiting for transfers between devices  16.4 us (7%)
  blocking collectives  10.8 us (4%)
    unnamed x68, local copies, waits for them, and re-layouts  34.8 us
    ppermute x4, starting transfers between devices, padded_2(): after = lax.ppermute(initial, axis, down)  20.5 us
    all_to_all x1, waiting for transfers between devices, relay_surface(): lax.all_to_all(outgoing, 'gx', split_axis=0, concat_axis=0, tiled=True)  16.4 us
    all_to_all x2, starting transfers between devices, mirror_row(): lax.all_to_all(spread[:, :, ::-1, :], 'gx', split_axis=2, concat_axis=2,...  12.5 us
    concatenate x2, other arithmetic, advance(): jnp.concatenate([fields, velocity[1:2]], axis=0)  12.3 us
    all_to_all x2, starting transfers between devices, mirror_row(): lax.all_to_all(split_rows, 'gx', split_axis=2, concat_axis=2, tiled=True)  11.8 us
    mul x2, other arithmetic, advance(): north_all = north_all * keep_face  11.7 us
    max x4, other arithmetic, face_flux(): jnp.maximum(velocity, 0.0) * lower_cells  10.9 us
  transfers between devices with their start and end apart: 13, of which 1 were waited for; matrix products, arithmetic and copies ran while one was open for 31% of the time, Pallas kernels for 0%

commit v1 on v0

v1 whole, which is shorter than its diff:
```python
import functools

import jax
import jax.numpy as jnp
from jax import lax
from jax.experimental import pallas as pl
from jax.experimental.pallas import tpu as pltpu
from jax.sharding import PartitionSpec as P

MESH = pl.DeviceIdType.MESH
LEVELS = 8
ROWS = 256
LANES = 128
STRIPS = 32
COLUMNS = 16
TOP = 7
CAP = 8
SLOTS = 64
FACES = 24
F32 = jnp.float32

warming_swell_coefficient = 0.1655
haline_base = 0.7655
warming_swell_quadratic = 0.05952
haline_curve = 0.00054914
warming_compression_coupling = 0.0001497
haline_press = 1.109e-05
mixing_contraction_coefficient = 0.0024341
lateral_mix = 0.08
mixing_base = 0.05
mixing_boost = 0.2


def density_at(heat, salt, level):
    depth = 10.0 * level + 5.0
    heat_one = -warming_swell_coefficient * (1.0 + warming_compression_coupling * depth)
    heat_two = -warming_swell_coefficient * 0.5 * warming_swell_quadratic
    salt_one = haline_base * (1.0 - haline_press * depth)
    salt_two = -haline_base * 0.5 * haline_curve
    return heat * (
        heat_one + heat_two * heat - mixing_contraction_coefficient * salt
    ) + salt * (salt_one + salt_two * salt)


def face_weights(speed):
    lower = jnp.maximum(speed, 0.0) + lateral_mix
    return lower, speed - lower


def face_flux(speed, lower_cells, upper_cells):
    lower, upper = face_weights(speed)
    return lower * lower_cells + upper * upper_cells


def sweep(x, speed, west, east, carry, mix, mask, first, last, resumed, dens, surf):
    lane = lax.broadcasted_iota(jnp.int32, (8, LANES), 1)
    sub = lax.broadcasted_iota(jnp.int32, (8, LANES), 0)
    first_lane, last_lane, first_row = lane == 0, lane == LANES - 1, sub == 0

    def advect(k, here, above, fw, fe, ocean):
        pu, qu, pv, qv = [], [], [], []
        for half in range(2):
            lower, upper = face_weights(speed[0, k, half, here, :])
            pu.append(lower)
            qu.append(upper)
            lower, upper = face_weights(speed[1, k, half, here, :])
            pv.append(lower)
            qv.append(upper)
        out = []
        for t in range(2):
            spot = t * LEVELS + k
            cells = [x[t, k, half, here, :] for half in range(2)]
            turned = [pltpu.roll(c, LANES - 1, 1) for c in cells]
            eastern = [jnp.where(last_lane, turned[1], turned[0]), turned[1]]
            ef = [pu[half] * cells[half] + qu[half] * eastern[half] for half in range(2)]
            ef[1] = jnp.where(last_lane, pltpu.roll(fe, LANES - 1 - spot, 1), ef[1])
            back = [pltpu.roll(f, 1, 1) for f in ef]
            edge = pltpu.roll(fw, LANES - spot, 1) if spot else fw
            wf = [jnp.where(first_lane, edge, back[0]), jnp.where(first_lane, back[0], back[1])]
            fields = []
            for half in range(2):
                nf = pv[half] * cells[half] + qv[half] * x[t, k, half, above, :]
                down = pltpu.roll(nf, 1, 0)
                sf = jnp.where(first_row, carry[t, k, half], down)
                carry[t, k, half] = down
                change = (ef[half] - wf[half]) + (nf - sf)
                fields.append(cells[half] - ocean[half] * change)
            out.append(fields)
        return out

    def strip(s, _):
        row = pl.multiple_of(s * 8, 8)
        here, above = pl.ds(row, 8), pl.ds(row + 1, 8)
        fw, fe = west[here, :], east[here, :]
        ocean = [mask[s, half].astype(F32) for half in range(2)]

        def settle(k, adv, flux, over):
            for half in range(2):
                done = []
                for t in range(2):
                    if flux is None:
                        gain = -over[t][half]
                    elif over is None:
                        gain = flux[t][half]
                    else:
                        gain = flux[t][half] - over[t][half]
                    value = adv[t][half] + ocean[half] * gain
                    x[t, k, half, here, :] = value
                    done.append(value)
                    if surf is not None and k == 0:
                        surf[2 * s + half, t] = value
                if dens is not None:
                    dens[k, half, here, :] = density_at(done[0], done[1], k)

        over = None
        if resumed:
            adv = [[x[t, first, half, here, :] for half in range(2)] for t in range(2)]
            over = [[mix[t, half, here, :] for half in range(2)] for t in range(2)]
        else:
            adv = advect(first, here, above, fw, fe, ocean)
        rho = [density_at(adv[0][half], adv[1][half], first) for half in range(2)]
        for k in range(first + 1, last + 1):
            lower = advect(k, here, above, fw, fe, ocean)
            rho_lower = [density_at(lower[0][half], lower[1][half], k) for half in range(2)]
            flux = [[None, None], [None, None]]
            for half in range(2):
                kappa = (mixing_base + 0.5 * mixing_boost) - 0.5 * mixing_boost * jnp.tanh(
                    rho_lower[half] - rho[half]
                )
                for t in range(2):
                    flux[t][half] = kappa * (lower[t][half] - adv[t][half])
            settle(k - 1, adv, flux, over)
            adv, rho, over = lower, rho_lower, flux
        if last == LEVELS - 1:
            settle(last, adv, None, over)
        else:
            for t in range(2):
                for half in range(2):
                    x[t, last, half, here, :] = adv[t][half]
                    mix[t, half, here, :] = over[t][half]
        return 0

    lax.fori_loop(0, STRIPS, strip, 0)


def pack(x, speed, e, levels, cols, rows):
    lane = lax.broadcasted_iota(jnp.int32, (8, LANES), 1)

    def group(g, _):
        to_east = jnp.zeros((8, LANES), F32)
        to_west = jnp.zeros((8, LANES), F32)
        for q in range(4):
            here = pl.ds(pl.multiple_of(g * 32 + q * 8, 8), 8)
            for k in levels:
                for t in range(2):
                    spot = 32 * q + t * LEVELS + k
                    value = pltpu.roll(x[t, k, 1, here, :], (spot + 1) % LANES, 1)
                    to_east = jnp.where(lane == spot, value, to_east)
                    value = x[t, k, 0, here, :]
                    if spot:
                        value = pltpu.roll(value, spot, 1)
                    to_west = jnp.where(lane == spot, value, to_west)
                for t in range(2):
                    spot = 32 * q + 16 + t * LEVELS + k
                    value = pltpu.roll(speed[0, k, 1, here, :], (spot + 1) % LANES, 1)
                    to_east = jnp.where(lane == spot, value, to_east)
        here = pl.ds(pl.multiple_of(g * 8, 8), 8)
        cols[e, 0, here, :] = to_east
        cols[e, 1, here, :] = to_west
        return 0

    lax.fori_loop(0, 8, group, 0)
    for k in levels:
        for half in range(2):
            for t in range(2):
                spot = t * 16 + k * 2 + half
                rows[e, 0, spot : spot + 1, :] = x[t, k, half, ROWS - 1 : ROWS, :]
                rows[e, 1, spot : spot + 1, :] = x[t, k, half, 0:1, :]
            spot = 32 + k * 2 + half
            rows[e, 0, spot : spot + 1, :] = speed[1, k, half, ROWS - 1 : ROWS, :]


def reversed_lanes(value):
    lane = lax.broadcasted_iota(jnp.int32, value.shape, 1)
    for bit in (1, 2, 4, 8, 16, 32, 64):
        upper = (lane & bit) != 0
        value = jnp.where(
            upper, pltpu.roll(value, bit, 1), pltpu.roll(value, LANES - bit, 1)
        )
    return value


def unpack(x, e, levels, cols, rows, cols_in, rows_in, west, east, carry, folded, top, open_south):
    def group(g, _):
        here = pl.ds(pl.multiple_of(g * 8, 8), 8)
        arrived, own = cols_in[e, 0, here, :], cols[e, 1, here, :]
        fw = face_flux(pltpu.roll(arrived, LANES - 16, 1), arrived, own)
        arrived, own = cols_in[e, 1, here, :], cols[e, 0, here, :]
        fe = face_flux(pltpu.roll(own, LANES - 16, 1), own, arrived)
        for q in range(4):
            here = pl.ds(pl.multiple_of(g * 32 + q * 8, 8), 8)
            west[here, :] = pltpu.roll(fw, LANES - 32 * q, 1) if q else fw
            east[here, :] = pltpu.roll(fe, LANES - 32 * q, 1) if q else fe
        return 0

    lax.fori_loop(0, 8, group, 0)
    speed = rows_in[e, 1, 32:48, :]
    for t in range(2):
        flux = face_flux(
            speed, rows_in[e, 1, 16 * t : 16 * t + 16, :], rows[e, 1, 16 * t : 16 * t + 16, :]
        )
        folded[16 * t : 16 * t + 16, :] = jnp.where(open_south, flux, 0.0)
    for k in levels:
        for half in range(2):
            for t in range(2):
                spot = t * 16 + k * 2 + half
                carry[t, k, half, 0:1, :] = folded[spot : spot + 1, :]

    @pl.when(top == 0)
    def _():
        folded[...] = rows_in[e, 0, 0:32, :]

    @pl.when(top == 1)
    def _():
        value = reversed_lanes(rows_in[e, 0, 0:32, :])
        odd = (lax.broadcasted_iota(jnp.int32, (32, LANES), 0) & 1) != 0
        folded[...] = jnp.where(odd, pltpu.roll(value, 1, 0), pltpu.roll(value, 31, 0))

    for k in levels:
        for half in range(2):
            for t in range(2):
                spot = t * 16 + k * 2 + half
                x[t, k, half, ROWS : ROWS + 1, :] = folded[spot : spot + 1, :]


def running_count(flags):
    lane = lax.broadcasted_iota(jnp.int32, flags.shape, 1)
    total = flags
    for shift in (1, 2, 4, 8, 16, 32):
        total = total + jnp.where(lane >= shift, pltpu.roll(total, shift, 1), 0)
    return total - flags


def lane_total(value):
    for shift in (1, 2, 4, 8, 16, 32, 64):
        value = value + pltpu.roll(value, shift, 1)
    return value


def send_table(lists, gx, stage, table):
    for p in range(COLUMNS):
        stage[p : p + 1, :] = lists[p, 0:1, :]
    ids = stage[...]
    lane = lax.broadcasted_iota(jnp.int32, ids.shape, 1)
    mine = ((ids & 31) >> 1 == gx) & (ids >= 0)
    rank = running_count(jnp.where(mine, 1, 0))
    tile = ((ids >> 5) & (STRIPS - 1)) * 2 + (ids & 1)
    out = jnp.zeros_like(ids)
    for r in range(CAP):
        found = lane_total(jnp.where(mine & (rank == r), tile, 0))
        out = jnp.where(lane == r, found, out)
    table[...] = out


def pick_table(lists, gx, out):
    ids = jnp.broadcast_to(lists[gx, 0:1, :], (COLUMNS, LANES))
    row = lax.broadcasted_iota(jnp.int32, ids.shape, 0)
    mine = ((ids & 31) >> 1 == row) & (ids >= 0)
    flags = jnp.where(mine, 1, 0)
    place = jnp.where(mine, running_count(flags) + row * CAP + 1, 0)
    both = place[0:8] + place[8:16]
    for shift in (4, 2, 1):
        both = both + pltpu.roll(both, shift, 0)
    out[...] = both - 1


def ocean_kernel(
    tracers, speeds, mask, own_list, x, dens, incoming, picks,
    speed, cols, rows, cols_in, rows_in, west, east, carry, mix, folded,
    lists, stage, table, table_s, surf, outgoing,
    load_sem, send_sem, recv_sem, list_send, list_recv, relay_send, relay_recv, local_sem,
):
    gy, gx = lax.axis_index("gy"), lax.axis_index("gx")
    top = gy // TOP
    inner = (gy + TOP - 1) // TOP
    east_at = lax.rem(gx + 1, COLUMNS)
    west_at = lax.rem(gx + COLUMNS - 1, COLUMNS)
    north_row = gy + 1 - top
    north_col = gx + top * (COLUMNS - 1 - 2 * gx)

    barrier = pltpu.get_barrier_semaphore()

    def greet(d, _):
        peer = lax.rem(gx + 1 + d, COLUMNS)
        pl.semaphore_signal(barrier, inc=1, device_id=(gy, peer), device_id_type=MESH)
        return 0

    lax.fori_loop(0, COLUMNS - 1, greet, 0)

    @pl.when(gy < TOP)
    def _():
        pl.semaphore_signal(barrier, inc=1, device_id=(gy + 1, gx), device_id_type=MESH)

    @pl.when(gy > 0)
    def _():
        pl.semaphore_signal(barrier, inc=1, device_id=(gy - 1, gx), device_id_type=MESH)

    def load_x(i, lo, hi):
        return [
            pltpu.make_async_copy(
                tracers.at[:, pl.ds(lo, hi - lo), :, pl.ds(half * LANES, LANES)],
                x.at[:, pl.ds(lo, hi - lo), half, pl.ds(0, ROWS), :],
                load_sem.at[i, half],
            )
            for half in range(2)
        ]

    def load_speed(i, step, lo, hi):
        return [
            pltpu.make_async_copy(
                speeds.at[step, :, pl.ds(lo, hi - lo), :, pl.ds(half * LANES, LANES)],
                speed.at[step, :, pl.ds(lo, hi - lo), half],
                load_sem.at[i, half],
            )
            for half in range(2)
        ]

    early = load_x(0, 0, 3) + load_speed(1, 0, 0, 3) + load_x(2, 3, 8) + load_speed(3, 0, 3, 8)
    late_low = load_speed(4, 1, 0, 2)
    late_high = load_speed(5, 1, 2, 8)
    for c in early + late_low + late_high:
        c.start()

    lists[gx] = jnp.full((8, LANES), -1, jnp.int32)
    lists[gx, :, 0:SLOTS] = jnp.broadcast_to(own_list[...], (8, SLOTS))

    for c in early:
        c.wait()
    pack(x, speed.at[0], 0, range(LEVELS), cols, rows)

    pl.semaphore_wait(barrier, COLUMNS - 1 + (1 - top) + inner)

    def send_edges(e):
        return [
            pltpu.make_async_remote_copy(
                cols.at[e, 0], cols_in.at[e, 0], send_sem.at[e, 0], recv_sem.at[e, 0],
                device_id=(gy, east_at), device_id_type=MESH,
            ),
            pltpu.make_async_remote_copy(
                cols.at[e, 1], cols_in.at[e, 1], send_sem.at[e, 1], recv_sem.at[e, 1],
                device_id=(gy, west_at), device_id_type=MESH,
            ),
            pltpu.make_async_remote_copy(
                rows.at[e, 0], rows_in.at[e, 1 - top], send_sem.at[e, 2], recv_sem.at[e, 3 - top],
                device_id=(north_row, north_col), device_id_type=MESH,
            ),
        ]

    def send_south(e):
        return pltpu.make_async_remote_copy(
            rows.at[e, 1], rows_in.at[e, 0], send_sem.at[e, 3], recv_sem.at[e, 2],
            device_id=(gy - 1, gx), device_id_type=MESH,
        )

    def start_edges(e):
        for c in send_edges(e):
            c.start()

        @pl.when(gy > 0)
        def _():
            send_south(e).start()

    def wait_edges(e):
        to_east, to_west, to_north = send_edges(e)
        to_east.wait_recv()
        to_west.wait_recv()
        pltpu.make_async_remote_copy(
            rows.at[e, 0], rows_in.at[e, 0], send_sem.at[e, 2], recv_sem.at[e, 2],
            device_id=(north_row, north_col), device_id_type=MESH,
        ).wait_recv()

        @pl.when(gy > 0)
        def _():
            pltpu.make_async_remote_copy(
                rows.at[e, 0], rows_in.at[e, 1], send_sem.at[e, 2], recv_sem.at[e, 3],
                device_id=(north_row, north_col), device_id_type=MESH,
            ).wait_recv()

    def finish_edges(e):
        for c in send_edges(e):
            c.wait_send()

        @pl.when(gy > 0)
        def _():
            send_south(e).wait_send()

    start_edges(0)

    def list_copy(peer, slot):
        return pltpu.make_async_remote_copy(
            lists.at[gx], lists.at[slot], list_send.at[peer], list_recv.at[slot],
            device_id=(gy, peer), device_id_type=MESH,
        )

    def send_list(d, _):
        list_copy(lax.rem(gx + 1 + d, COLUMNS), gx).start()
        return 0

    lax.fori_loop(0, COLUMNS - 1, send_list, 0)

    def fill(e, levels):
        wait_edges(e)
        unpack(x, e, levels, cols, rows, cols_in, rows_in, west, east, carry, folded, top, gy > 0)

    fill(0, range(LEVELS))
    sweep(x, speed.at[0], west, east, carry, mix, mask, 0, 2, False, None, None)
    for c in late_low:
        c.wait()
    pack(x, speed.at[1], 1, range(0, 2), cols, rows)
    start_edges(1)
    sweep(x, speed.at[0], west, east, carry, mix, mask, 2, 7, True, None, None)
    for c in late_high:
        c.wait()
    pack(x, speed.at[1], 2, range(2, 8), cols, rows)
    start_edges(2)

    def take_list(d, _):
        peer = lax.rem(gx + 1 + d, COLUMNS)
        list_copy(peer, peer).wait_recv()
        return 0

    lax.fori_loop(0, COLUMNS - 1, take_list, 0)
    send_table(lists, gx, stage, table)
    fetch = pltpu.make_async_copy(table, table_s, local_sem)
    fetch.start()
    pick_table(lists, gx, picks)

    fill(1, range(0, 2))
    sweep(x, speed.at[1], west, east, carry, mix, mask, 0, 1, False, dens, surf)
    fetch.wait()

    def bucket(peer, target, base):
        def slot(r, _):
            tile = jnp.clip(table_s[peer, r], 0, SLOTS - 1)
            target[base + r] = surf[tile]
            return 0

        lax.fori_loop(0, CAP, slot, 0)

    def relay_copy(peer, slot):
        return pltpu.make_async_remote_copy(
            outgoing.at[pl.ds(peer * CAP, CAP)], incoming.at[pl.ds(slot * CAP, CAP)],
            relay_send.at[peer], relay_recv.at[slot],
            device_id=(gy, peer), device_id_type=MESH,
        )

    def relay(d, _):
        peer = lax.rem(gx + 1 + lax.rem(d + 7, COLUMNS - 1), COLUMNS)
        bucket(peer, outgoing, peer * CAP)
        relay_copy(peer, gx).start()
        return 0

    lax.fori_loop(0, COLUMNS - 1, relay, 0)
    bucket(gx, incoming, gx * CAP)

    fill(2, range(2, 8))
    sweep(x, speed.at[1], west, east, carry, mix, mask, 1, 7, True, dens, None)

    for e in range(3):
        finish_edges(e)

    def close(d, _):
        peer = lax.rem(gx + 1 + d, COLUMNS)
        list_copy(peer, gx).wait_send()
        relay_copy(peer, gx).wait_send()
        relay_copy(peer, peer).wait_recv()
        return 0

    lax.fori_loop(0, COLUMNS - 1, close, 0)


def output_kernel(x, dens, incoming, picks, tracers_out, dens_out, ice_out, ice, sems):
    copies = []
    for half in range(2):
        lanes = pl.ds(half * LANES, LANES)
        copies.append(
            pltpu.make_async_copy(
                x.at[:, :, half, pl.ds(0, ROWS), :], tracers_out.at[:, :, :, lanes], sems.at[half]
            )
        )
        copies.append(
            pltpu.make_async_copy(
                dens.at[:, half], dens_out.at[:, :, lanes], sems.at[2 + half]
            )
        )
    for c in copies:
        c.start()

    def slot(s, _):
        place = picks[0, s]
        filled = place >= 0
        spot = jnp.clip(place, 0, COLUMNS * CAP - 1)
        heat = jnp.where(filled, incoming[spot, 0], 0.0)
        salt = jnp.where(filled, incoming[spot, 1], 0.0)
        ice[s, 0] = heat
        ice[s, 1] = salt
        ice[s, 2] = density_at(heat, salt, 0)
        return 0

    for part in range(2):
        lax.fori_loop(part * 32, part * 32 + 32, slot, 0)
        c = pltpu.make_async_copy(
            ice.at[pl.ds(part * 32, 32)], ice_out.at[pl.ds(part * 32, 32)], sems.at[4 + part]
        )
        c.start()
        copies.append(c)
    for c in copies:
        c.wait()


def on_device(tracers, face_speeds, ocean_block, ice_blocks):
    anywhere = pl.BlockSpec(memory_space=pl.ANY)
    vmem = pl.BlockSpec(memory_space=pltpu.VMEM)
    smem = pl.BlockSpec(memory_space=pltpu.SMEM)
    dma = pltpu.SemaphoreType.DMA
    x, dens, incoming, picks = pl.pallas_call(
        ocean_kernel,
        out_shape=(
            jax.ShapeDtypeStruct((2, LEVELS, 2, ROWS + 8, LANES), F32),
            jax.ShapeDtypeStruct((LEVELS, 2, ROWS, LANES), F32),
            jax.ShapeDtypeStruct((COLUMNS * CAP, 2, 8, LANES), F32),
            jax.ShapeDtypeStruct((8, LANES), jnp.int32),
        ),
        in_specs=[anywhere, anywhere, smem, vmem],
        out_specs=(vmem, vmem, vmem, vmem),
        scratch_shapes=[
            pltpu.VMEM((2, 2, LEVELS, 2, ROWS, LANES), F32),
            pltpu.VMEM((3, 2, 64, LANES), F32),
            pltpu.VMEM((3, 2, 48, LANES), F32),
            pltpu.VMEM((3, 2, 64, LANES), F32),
            pltpu.VMEM((3, 2, 48, LANES), F32),
            pltpu.VMEM((ROWS, LANES), F32),
            pltpu.VMEM((ROWS, LANES), F32),
            pltpu.VMEM((2, LEVELS, 2, 8, LANES), F32),
            pltpu.VMEM((2, 2, ROWS, LANES), F32),
            pltpu.VMEM((32, LANES), F32),
            pltpu.VMEM((COLUMNS, 8, LANES), jnp.int32),
            pltpu.VMEM((COLUMNS, LANES), jnp.int32),
            pltpu.VMEM((COLUMNS, LANES), jnp.int32),
            pltpu.SMEM((COLUMNS, LANES), jnp.int32),
            pltpu.VMEM((SLOTS, 2, 8, LANES), F32),
            pltpu.VMEM((COLUMNS * CAP, 2, 8, LANES), F32),
            dma((6, 2)),
            dma((3, 4)),
            dma((3, 4)),
            dma((COLUMNS,)),
            dma((COLUMNS,)),
            dma((COLUMNS,)),
            dma((COLUMNS,)),
            dma,
        ],
        compiler_params=pltpu.CompilerParams(
            collective_id=0, has_side_effects=True, vmem_limit_bytes=48 << 20
        ),
        name="ocean",
    )(tracers, face_speeds, ocean_block, ice_blocks.reshape(1, SLOTS))
    return pl.pallas_call(
        output_kernel,
        out_shape=(
            jax.ShapeDtypeStruct(tracers.shape, F32),
            jax.ShapeDtypeStruct(tracers.shape[1:], F32),
            jax.ShapeDtypeStruct((SLOTS, 3, 8, LANES), F32),
        ),
        in_specs=[anywhere, anywhere, vmem, smem],
        out_specs=(anywhere, anywhere, anywhere),
        scratch_shapes=[pltpu.VMEM((SLOTS, 3, 8, LANES), F32), dma((6,))],
        compiler_params=pltpu.CompilerParams(vmem_limit_bytes=16 << 20),
        name="outputs",
    )(x, dens, incoming, picks)


def solution(mesh):
    return jax.shard_map(
        on_device,
        mesh=mesh,
        in_specs=(
            P(None, None, "gy", "gx"),
            P(None, None, None, "gy", "gx"),
            P("gy", "gx"),
            P(("gy", "gx")),
        ),
        out_specs=(
            P(None, None, "gy", "gx"),
            P(None, "gy", "gx"),
            P(("gy", "gx"), None, None, None),
        ),
        check_vma=False,
    )
```

time: 246 us -> 67.4 us (0.27)
  the two profiles are of different devices: /device:TPU:32 before, /device:TPU:39 now
where the time goes in v1:
time: 67.4 us; the launch traced here: 66.8 us
  Pallas kernels  62.5 us (93%)
  local copies, waits for them, and re-layouts  3.63 us (5%)
    pallas_call x1, Pallas kernels, on_device(): pl.pallas_call(ocean_kernel, out_shape=(jax.ShapeDtypeStruct((2, LEVELS,...  59 us
    unnamed x5, local copies, waits for them, and re-layouts  3.63 us
    pallas_call x1, Pallas kernels, on_device(): pl.pallas_call(output_kernel, out_shape=(jax.ShapeDtypeStruct(tracers.sha...  3.56 us

profile of v1, /device:TPU:39, one launch (start us, length us, event | category | flops | bytes accessed | tf_op | source)
XLA Modules:
  0.0 66.8 jit_solution(8417802500757395325)
XLA Ops:
  0.6 0.8 %copy.7.mask = s32[32,2]{1,0:T(8,128)S(1)} copy(s32[32,2]{0,1:T(2,128)} %param.6) | data formatting | bytes 512 | tf_op args[2]
  1.4 0.0 copy-start.1
  1.4 0.7 copy-done.1
  2.0 59.0 %ocean.1 = (f32[2,8,2,264,128]{4,3,2,1,0:T(8,128)}, f32[8,2,256,128]{3,2,1,0:T(8,128)S(1)}, f32[128,2,8,128]{3,2,1,0:T(8,128)S(1)}, s32[8,128]{1,0:T(8,128)S(1)}) custom-call(f32[2,8,256,256]{3,2,1,0:T(8,128)} %tracers.1, f32[2,2,8,256,256]{4,3,2,1,0:T(8,128)} %speeds.1, s32[32,2]{1,0:T(8,128)S(1)} %copy.7.mask, s32[1,64]{1,0:T(1,128)S(1)} %bitcast.1), custom_call_target="tpu_custom_call" | custom-call | tf_op jit(solution)/shard_map/ocean/pallas_call | solution.py:526
  61.0 0.0 copy-start
  61.0 2.2 %copy-done = f32[2,8,2,264,128]{4,3,2,1,0:T(8,128)S(1)} copy-done((f32[2,8,2,264,128]{4,3,2,1,0:T(8,128)S(1)}, f32[2,8,2,264,128]{4,3,2,1,0:T(8,128)}, u32[]{:S(2)}) %copy-start) | copy-done | bytes 4325400
  63.3 3.6 %outputs.1 = (f32[2,8,256,256]{3,2,1,0:T(8,128)}, f32[8,256,256]{2,1,0:T(8,128)}, f32[64,3,8,128]{3,2,1,0:T(8,128)}) custom-call(f32[2,8,2,264,128]{4,3,2,1,0:T(8,128)S(1)} %copy-done, f32[8,2,256,128]{3,2,1,0:T(8,128)S(1)} %get-tuple-element.8.dens, f32[128,2,8,128]{3,2,1,0:T(8,128)S(1)} %get-tuple-element.9.incoming, s32[8,128]{1,0:T(8,128)S(1)} %get-tuple-element.10.picks), custom_call_target="tpu_custom_call" | custom-call | tf_op jit(solution)/shard_map/outputs/pallas_call | solution.py:567
Async XLA Ops:
  1.4 0.7 copy-start.1
  61.0 2.2 %copy-start = (f32[2,8,2,264,128]{4,3,2,1,0:T(8,128)S(1)}, f32[2,8,2,264,128]{4,3,2,1,0:T(8,128)}, u32[]{:S(2)}) copy-start(f32[2,8,2,264,128]{4,3,2,1,0:T(8,128)} %get-tuple-element.7.x) | copy-start | bytes 12976132

commit v2 on v1

--- a/solution.py
+++ b/solution.py
@@ -12,6 +12,7 @@
 ROWS = 256
 LANES = 128
 STRIPS = 32
+CHUNK = 64
 COLUMNS = 16
 TOP = 7
 CAP = 8
@@ -52,47 +53,55 @@
     return lower * lower_cells + upper * upper_cells
 
 
-def sweep(x, speed, west, east, carry, mix, mask, first, last, resumed, dens, surf):
-    lane = lax.broadcasted_iota(jnp.int32, (8, LANES), 1)
-    sub = lax.broadcasted_iota(jnp.int32, (8, LANES), 0)
-    first_lane, last_lane, first_row = lane == 0, lane == LANES - 1, sub == 0
-
-    def advect(k, here, above, fw, fe, ocean):
-        pu, qu, pv, qv = [], [], [], []
-        for half in range(2):
-            lower, upper = face_weights(speed[0, k, half, here, :])
-            pu.append(lower)
-            qu.append(upper)
-            lower, upper = face_weights(speed[1, k, half, here, :])
-            pv.append(lower)
-            qv.append(upper)
-        out = []
+def advance(x, speed, ocean_v, low, high):
+    lane = lax.broadcasted_iota(jnp.int32, (ROWS, LANES), 1)
+    first_lane, last_lane = lane == 0, lane == LANES - 1
+    last_row = lax.broadcasted_iota(jnp.int32, (8, LANES), 0) == 7
+    here, above = pl.ds(0, ROWS), pl.ds(1, ROWS)
+
+    def level(k, _):
+        east = [face_weights(speed[0, k, half]) for half in range(2)]
+        north = [face_weights(speed[1, k, half]) for half in range(2)]
         for t in range(2):
-            spot = t * LEVELS + k
             cells = [x[t, k, half, here, :] for half in range(2)]
             turned = [pltpu.roll(c, LANES - 1, 1) for c in cells]
             eastern = [jnp.where(last_lane, turned[1], turned[0]), turned[1]]
-            ef = [pu[half] * cells[half] + qu[half] * eastern[half] for half in range(2)]
-            ef[1] = jnp.where(last_lane, pltpu.roll(fe, LANES - 1 - spot, 1), ef[1])
+            ef = [east[half][0] * cells[half] + east[half][1] * eastern[half] for half in range(2)]
+            ef[1] = jnp.where(last_lane, 0.0, ef[1])
             back = [pltpu.roll(f, 1, 1) for f in ef]
-            edge = pltpu.roll(fw, LANES - spot, 1) if spot else fw
-            wf = [jnp.where(first_lane, edge, back[0]), jnp.where(first_lane, back[0], back[1])]
-            fields = []
+            wf = [jnp.where(first_lane, 0.0, back[0]), jnp.where(first_lane, back[0], back[1])]
             for half in range(2):
-                nf = pv[half] * cells[half] + qv[half] * x[t, k, half, above, :]
-                down = pltpu.roll(nf, 1, 0)
-                sf = jnp.where(first_row, carry[t, k, half], down)
-                carry[t, k, half] = down
-                change = (ef[half] - wf[half]) + (nf - sf)
-                fields.append(cells[half] - ocean[half] * change)
-            out.append(fields)
-        return out
-
-    def strip(s, _):
-        row = pl.multiple_of(s * 8, 8)
-        here, above = pl.ds(row, 8), pl.ds(row + 1, 8)
-        fw, fe = west[here, :], east[here, :]
-        ocean = [mask[s, half].astype(F32) for half in range(2)]
+                nf = north[half][0] * cells[half] + north[half][1] * x[t, k, half, above, :]
+                nf = jnp.concatenate(
+                    [nf[: ROWS - 8], jnp.where(last_row, 0.0, nf[ROWS - 8 :])], axis=0
+                )
+                change = (ef[half] - wf[half]) + (nf - pltpu.roll(nf, 1, 0))
+                x[t, k, half, here, :] = cells[half] - ocean_v[half] * change
+        return 0
+
+    lax.fori_loop(low, high, level, 0)
+
+
+def settle_levels(x, edge, mix, ocean_v, first, last, resumed, dens, surf):
+    lane = lax.broadcasted_iota(jnp.int32, (CHUNK, LANES), 1)
+    first_lane, last_lane = lane == 0, lane == LANES - 1
+
+    def chunk(c, _):
+        here = pl.ds(pl.multiple_of(c * CHUNK, CHUNK), CHUNK)
+        rim = edge[here, :]
+        ocean = [ocean_v[half, here, :] for half in range(2)]
+
+        def advected(k):
+            out = []
+            for t in range(2):
+                ends = pltpu.roll(rim, LANES - 1 - 2 * (t * LEVELS + k), 1)
+                out.append(
+                    [
+                        x[t, k, 0, here, :] + jnp.where(first_lane, ends, 0.0),
+                        x[t, k, 1, here, :] + jnp.where(last_lane, ends, 0.0),
+                    ]
+                )
+            return out
 
         def settle(k, adv, flux, over):
             for half in range(2):
@@ -108,7 +117,9 @@
                     x[t, k, half, here, :] = value
                     done.append(value)
                     if surf is not None and k == 0:
-                        surf[2 * s + half, t] = value
+                        for i in range(CHUNK // 8):
+                            tile = 2 * (c * (CHUNK // 8) + i) + half
+                            surf[tile, t] = value[8 * i : 8 * i + 8]
                 if dens is not None:
                     dens[k, half, here, :] = density_at(done[0], done[1], k)
 
@@ -117,10 +128,10 @@
             adv = [[x[t, first, half, here, :] for half in range(2)] for t in range(2)]
             over = [[mix[t, half, here, :] for half in range(2)] for t in range(2)]
         else:
-            adv = advect(first, here, above, fw, fe, ocean)
+            adv = advected(first)
         rho = [density_at(adv[0][half], adv[1][half], first) for half in range(2)]
         for k in range(first + 1, last + 1):
-            lower = advect(k, here, above, fw, fe, ocean)
+            lower = advected(k)
             rho_lower = [density_at(lower[0][half], lower[1][half], k) for half in range(2)]
             flux = [[None, None], [None, None]]
             for half in range(2):
@@ -140,36 +151,47 @@
                     mix[t, half, here, :] = over[t][half]
         return 0
 
-    lax.fori_loop(0, STRIPS, strip, 0)
+    lax.fori_loop(0, ROWS // CHUNK, chunk, 0)
+
+
+def aligned(index):
+    return index if isinstance(index, int) else pl.multiple_of(index, 8)
 
 
 def pack(x, speed, e, levels, cols, rows):
     lane = lax.broadcasted_iota(jnp.int32, (8, LANES), 1)
 
     def group(g, _):
-        to_east = jnp.zeros((8, LANES), F32)
-        to_west = jnp.zeros((8, LANES), F32)
+        parts = []
         for q in range(4):
-            here = pl.ds(pl.multiple_of(g * 32 + q * 8, 8), 8)
+            here = pl.ds(aligned(g * 32 + q * 8), 8)
+            east = jnp.zeros((8, LANES), F32)
+            west = jnp.zeros((8, LANES), F32)
+            face = jnp.zeros((8, LANES), F32)
             for k in levels:
                 for t in range(2):
-                    spot = 32 * q + t * LEVELS + k
-                    value = pltpu.roll(x[t, k, 1, here, :], (spot + 1) % LANES, 1)
-                    to_east = jnp.where(lane == spot, value, to_east)
-                    value = x[t, k, 0, here, :]
-                    if spot:
-                        value = pltpu.roll(value, spot, 1)
-                    to_west = jnp.where(lane == spot, value, to_west)
-                for t in range(2):
-                    spot = 32 * q + 16 + t * LEVELS + k
-                    value = pltpu.roll(speed[0, k, 1, here, :], (spot + 1) % LANES, 1)
-                    to_east = jnp.where(lane == spot, value, to_east)
-        here = pl.ds(pl.multiple_of(g * 8, 8), 8)
-        cols[e, 0, here, :] = to_east
-        cols[e, 1, here, :] = to_west
-        return 0
-
-    lax.fori_loop(0, 8, group, 0)
+                    spot = 32 * q + 2 * (t * LEVELS + k)
+                    value = pltpu.roll(x[t, k, 1, here, :], spot + 1, 1)
+                    east = jnp.where(lane == spot, value, east)
+                    value = pltpu.roll(x[t, k, 0, here, :], spot + 1, 1)
+                    west = jnp.where(lane == spot + 1, value, west)
+                spot = 32 * q + 2 * k + 1
+                value = pltpu.roll(speed[0, k, 1, here, :], spot + 1, 1)
+                face = jnp.where(lane == spot, value, face)
+            parts.append((east, west, face))
+        east, west, face = [
+            (parts[0][i] + parts[1][i]) + (parts[2][i] + parts[3][i]) for i in range(3)
+        ]
+        here = pl.ds(aligned(g * 8), 8)
+        cols[e, 0, here, :] = (east + face) + pltpu.roll(face, 2 * LEVELS, 1)
+        cols[e, 1, here, :] = west
+        return 0
+
+    if len(levels) <= 3:
+        for g in range(8):
+            group(g, 0)
+    else:
+        lax.fori_loop(0, 8, group, 0, unroll=2)
     for k in levels:
         for half in range(2):
             for t in range(2):
@@ -190,47 +212,51 @@
     return value
 
 
-def unpack(x, e, levels, cols, rows, cols_in, rows_in, west, east, carry, folded, top, open_south):
-    def group(g, _):
-        here = pl.ds(pl.multiple_of(g * 8, 8), 8)
-        arrived, own = cols_in[e, 0, here, :], cols[e, 1, here, :]
-        fw = face_flux(pltpu.roll(arrived, LANES - 16, 1), arrived, own)
-        arrived, own = cols_in[e, 1, here, :], cols[e, 0, here, :]
-        fe = face_flux(pltpu.roll(own, LANES - 16, 1), own, arrived)
+def unpack(x, e, levels, cols, rows, cols_in, rows_in, edge, ocean_v, flows, top, open_south):
+    odd = (lax.broadcasted_iota(jnp.int32, (8, LANES), 1) & 1) != 0
+    for g in range(8):
+        here = pl.ds(g * 8, 8)
+        arrived = cols_in[e, 0, here, :]
+        fw = face_flux(arrived, pltpu.roll(arrived, 1, 1), cols[e, 1, here, :])
+        own, arrived = cols[e, 0, here, :], cols_in[e, 1, here, :]
+        fe = face_flux(pltpu.roll(own, LANES - 1, 1), own, pltpu.roll(arrived, LANES - 1, 1))
+        both = jnp.where(odd, fw, -fe)
         for q in range(4):
-            here = pl.ds(pl.multiple_of(g * 32 + q * 8, 8), 8)
-            west[here, :] = pltpu.roll(fw, LANES - 32 * q, 1) if q else fw
-            east[here, :] = pltpu.roll(fe, LANES - 32 * q, 1) if q else fe
-        return 0
-
-    lax.fori_loop(0, 8, group, 0)
+            here = pl.ds(g * 32 + q * 8, 8)
+            ocean = jnp.where(odd, ocean_v[0, here, :], ocean_v[1, here, :])
+            edge[e, here, :] = (pltpu.roll(both, LANES - 32 * q, 1) if q else both) * ocean
+
+    right = (lax.broadcasted_iota(jnp.int32, (16, LANES), 0) & 1) != 0
+    low = jnp.where(right, ocean_v[1, 0:1, :], ocean_v[0, 0:1, :])
+    high = jnp.where(right, ocean_v[1, ROWS - 1 : ROWS, :], ocean_v[0, ROWS - 1 : ROWS, :])
     speed = rows_in[e, 1, 32:48, :]
     for t in range(2):
-        flux = face_flux(
-            speed, rows_in[e, 1, 16 * t : 16 * t + 16, :], rows[e, 1, 16 * t : 16 * t + 16, :]
-        )
-        folded[16 * t : 16 * t + 16, :] = jnp.where(open_south, flux, 0.0)
+        part = pl.ds(16 * t, 16)
+        flux = face_flux(speed, rows_in[e, 1, part, :], rows[e, 1, part, :])
+        flows[0, part, :] = jnp.where(open_south, low * flux, 0.0)
+
+    def north(arrived):
+        for t in range(2):
+            part = pl.ds(16 * t, 16)
+            flux = face_flux(rows[e, 0, 32:48, :], rows[e, 0, part, :], arrived[16 * t : 16 * t + 16])
+            flows[1, part, :] = -high * flux
+
+    @pl.when(top == 0)
+    def _():
+        north(rows_in[e, 0, 0:32, :])
+
+    @pl.when(top == 1)
+    def _():
+        value = reversed_lanes(rows_in[e, 0, 0:32, :])
+        odd_row = (lax.broadcasted_iota(jnp.int32, (32, LANES), 0) & 1) != 0
+        north(jnp.where(odd_row, pltpu.roll(value, 1, 0), pltpu.roll(value, 31, 0)))
+
     for k in levels:
         for half in range(2):
             for t in range(2):
                 spot = t * 16 + k * 2 + half
-                carry[t, k, half, 0:1, :] = folded[spot : spot + 1, :]
-
-    @pl.when(top == 0)
-    def _():
-        folded[...] = rows_in[e, 0, 0:32, :]
-
-    @pl.when(top == 1)
-    def _():
-        value = reversed_lanes(rows_in[e, 0, 0:32, :])
-        odd = (lax.broadcasted_iota(jnp.int32, (32, LANES), 0) & 1) != 0
-        folded[...] = jnp.where(odd, pltpu.roll(value, 1, 0), pltpu.roll(value, 31, 0))
-
-    for k in levels:
-        for half in range(2):
-            for t in range(2):
-                spot = t * 16 + k * 2 + half
-                x[t, k, half, ROWS : ROWS + 1, :] = folded[spot : spot + 1, :]
+                x[t, k, half, 0:1, :] += flows[0, spot : spot + 1, :]
+                x[t, k, half, ROWS - 1 : ROWS, :] += flows[1, spot : spot + 1, :]
 
 
 def running_count(flags):
@@ -275,8 +301,8 @@
 
 
 def ocean_kernel(
-    tracers, speeds, mask, own_list, x, dens, incoming, picks,
-    speed, cols, rows, cols_in, rows_in, west, east, carry, mix, folded,
+    tracers, speeds, land, own_list, x, dens, incoming, picks,
+    speed, cols, rows, cols_in, rows_in, edge, mix, ocean_v, flows, own_v, mask,
     lists, stage, table, table_s, surf, outgoing,
     load_sem, send_sem, recv_sem, list_send, list_recv, relay_send, relay_recv, local_sem,
 ):
@@ -325,20 +351,24 @@
             for half in range(2)
         ]
 
-    early = load_x(0, 0, 3) + load_speed(1, 0, 0, 3) + load_x(2, 3, 8) + load_speed(3, 0, 3, 8)
+    own = pltpu.make_async_copy(own_list, own_v, local_sem.at[0])
+    own.start()
+    blocks = pltpu.make_async_copy(land, mask, local_sem.at[1])
+    blocks.start()
+    upper = load_x(0, 0, 3) + load_speed(1, 0, 0, 3)
+    deep = load_x(2, 3, 8) + load_speed(3, 0, 3, 8)
     late_low = load_speed(4, 1, 0, 2)
     late_high = load_speed(5, 1, 2, 8)
-    for c in early + late_low + late_high:
+    for c in upper + deep + late_low + late_high:
         c.start()
 
+    blocks.wait()
+    for half in range(2):
+        for s in range(STRIPS):
+            ocean_v[half, 8 * s : 8 * s + 8, :] = jnp.full((8, LANES), mask[half, s].astype(F32))
+    own.wait()
     lists[gx] = jnp.full((8, LANES), -1, jnp.int32)
-    lists[gx, :, 0:SLOTS] = jnp.broadcast_to(own_list[...], (8, SLOTS))
-
-    for c in early:
-        c.wait()
-    pack(x, speed.at[0], 0, range(LEVELS), cols, rows)
-
-    pl.semaphore_wait(barrier, COLUMNS - 1 + (1 - top) + inner)
+    lists[gx, :, 0:SLOTS] = jnp.broadcast_to(own_v[...], (8, SLOTS))
 
     def send_edges(e):
         return [
@@ -371,9 +401,11 @@
             send_south(e).start()
 
     def wait_edges(e):
-        to_east, to_west, to_north = send_edges(e)
-        to_east.wait_recv()
-        to_west.wait_recv()
+        for side, peer in ((0, east_at), (1, west_at)):
+            pltpu.make_async_remote_copy(
+                cols.at[e, side], cols_in.at[e, side], send_sem.at[e, side], recv_sem.at[e, side],
+                device_id=(gy, peer), device_id_type=MESH,
+            ).wait_recv()
         pltpu.make_async_remote_copy(
             rows.at[e, 0], rows_in.at[e, 0], send_sem.at[e, 2], recv_sem.at[e, 2],
             device_id=(north_row, north_col), device_id_type=MESH,
@@ -394,6 +426,11 @@
         def _():
             send_south(e).wait_send()
 
+    for c in upper:
+        c.wait()
+    pack(x, speed.at[0], 0, range(0, 3), cols, rows)
+    advance(x, speed.at[0], ocean_v, 0, 3)
+    pl.semaphore_wait(barrier, COLUMNS - 1 + (1 - top) + inner)
     start_edges(0)
 
     def list_copy(peer, slot):
@@ -410,19 +447,31 @@
 
     def fill(e, levels):
         wait_edges(e)
-        unpack(x, e, levels, cols, rows, cols_in, rows_in, west, east, carry, folded, top, gy > 0)
-
-    fill(0, range(LEVELS))
-    sweep(x, speed.at[0], west, east, carry, mix, mask, 0, 2, False, None, None)
+        unpack(x, e, levels, cols, rows, cols_in, rows_in, edge, ocean_v, flows, top, gy > 0)
+
+    def settle(e, m, first, last, resumed, dens_ref, surf_ref):
+        settle_levels(x, edge.at[e], mix.at[m], ocean_v, first, last, resumed, dens_ref, surf_ref)
+
+    for c in deep:
+        c.wait()
+    pack(x, speed.at[0], 1, range(3, 8), cols, rows)
+    start_edges(1)
+    advance(x, speed.at[0], ocean_v, 3, 8)
+
+    fill(0, range(0, 3))
+    settle(0, 0, 0, 2, False, None, None)
     for c in late_low:
         c.wait()
-    pack(x, speed.at[1], 1, range(0, 2), cols, rows)
-    start_edges(1)
-    sweep(x, speed.at[0], west, east, carry, mix, mask, 2, 7, True, None, None)
+    pack(x, speed.at[1], 2, range(0, 2), cols, rows)
+    start_edges(2)
+    advance(x, speed.at[1], ocean_v, 0, 2)
+
+    fill(1, range(3, 8))
+    settle(1, 0, 2, 7, True, None, None)
     for c in late_high:
         c.wait()
-    pack(x, speed.at[1], 2, range(2, 8), cols, rows)
-    start_edges(2)
+    pack(x, speed.at[1], 3, range(2, 8), cols, rows)
+    start_edges(3)
 
     def take_list(d, _):
         peer = lax.rem(gx + 1 + d, COLUMNS)
@@ -431,21 +480,19 @@
 
     lax.fori_loop(0, COLUMNS - 1, take_list, 0)
     send_table(lists, gx, stage, table)
-    fetch = pltpu.make_async_copy(table, table_s, local_sem)
+    fetch = pltpu.make_async_copy(table, table_s, local_sem.at[1])
     fetch.start()
     pick_table(lists, gx, picks)
 
-    fill(1, range(0, 2))
-    sweep(x, speed.at[1], west, east, carry, mix, mask, 0, 1, False, dens, surf)
+    fill(2, range(0, 2))
+    settle(2, 1, 0, 1, False, dens, surf)
     fetch.wait()
 
     def bucket(peer, target, base):
-        def slot(r, _):
-            tile = jnp.clip(table_s[peer, r], 0, SLOTS - 1)
-            target[base + r] = surf[tile]
-            return 0
-
-        lax.fori_loop(0, CAP, slot, 0)
+        tiles = [jnp.clip(table_s[peer, r], 0, SLOTS - 1) for r in range(CAP)]
+        blocks = [surf[tile] for tile in tiles]
+        for r in range(CAP):
+            target[base + r] = blocks[r]
 
     def relay_copy(peer, slot):
         return pltpu.make_async_remote_copy(
@@ -454,19 +501,27 @@
             device_id=(gy, peer), device_id_type=MESH,
         )
 
-    def relay(d, _):
-        peer = lax.rem(gx + 1 + lax.rem(d + 7, COLUMNS - 1), COLUMNS)
+    def relay_far(d, _):
+        peer = (1 - gx // 8) * 8 + lax.rem(gx + d, 8)
         bucket(peer, outgoing, peer * CAP)
         relay_copy(peer, gx).start()
         return 0
 
-    lax.fori_loop(0, COLUMNS - 1, relay, 0)
+    def relay_near(d, _):
+        peer = (gx // 8) * 8 + lax.rem(gx + 1 + d, 8)
+        bucket(peer, outgoing, peer * CAP)
+        relay_copy(peer, gx).start()
+        return 0
+
+    lax.fori_loop(0, 8, relay_far, 0)
+    lax.fori_loop(0, 7, relay_near, 0)
     bucket(gx, incoming, gx * CAP)
 
-    fill(2, range(2, 8))
-    sweep(x, speed.at[1], west, east, carry, mix, mask, 1, 7, True, dens, None)
-
-    for e in range(3):
+    advance(x, speed.at[1], ocean_v, 2, 8)
+    fill(3, range(2, 8))
+    settle(3, 1, 1, 7, True, dens, None)
+
+    for e in range(4):
         finish_edges(e)
 
     def close(d, _):
@@ -508,7 +563,7 @@
         return 0
 
     for part in range(2):
-        lax.fori_loop(part * 32, part * 32 + 32, slot, 0)
+        lax.fori_loop(part * 32, part * 32 + 32, slot, 0, unroll=8)
         c = pltpu.make_async_copy(
             ice.at[pl.ds(part * 32, 32)], ice_out.at[pl.ds(part * 32, 32)], sems.at[4 + part]
         )
@@ -522,6 +577,7 @@
     anywhere = pl.BlockSpec(memory_space=pl.ANY)
     vmem = pl.BlockSpec(memory_space=pltpu.VMEM)
     smem = pl.BlockSpec(memory_space=pltpu.SMEM)
+    hbm = pl.BlockSpec(memory_space=pltpu.HBM)
     dma = pltpu.SemaphoreType.DMA
     x, dens, incoming, picks = pl.pallas_call(
         ocean_kernel,
@@ -531,19 +587,20 @@
             jax.ShapeDtypeStruct((COLUMNS * CAP, 2, 8, LANES), F32),
             jax.ShapeDtypeStruct((8, LANES), jnp.int32),
         ),
-        in_specs=[anywhere, anywhere, smem, vmem],
+        in_specs=[hbm, hbm, hbm, hbm],
         out_specs=(vmem, vmem, vmem, vmem),
         scratch_shapes=[
             pltpu.VMEM((2, 2, LEVELS, 2, ROWS, LANES), F32),
-            pltpu.VMEM((3, 2, 64, LANES), F32),
-            pltpu.VMEM((3, 2, 48, LANES), F32),
-            pltpu.VMEM((3, 2, 64, LANES), F32),
-            pltpu.VMEM((3, 2, 48, LANES), F32),
-            pltpu.VMEM((ROWS, LANES), F32),
-            pltpu.VMEM((ROWS, LANES), F32),
-            pltpu.VMEM((2, LEVELS, 2, 8, LANES), F32),
-            pltpu.VMEM((2, 2, ROWS, LANES), F32),
-            pltpu.VMEM((32, LANES), F32),
+            pltpu.VMEM((4, 2, 64, LANES), F32),
+            pltpu.VMEM((4, 2, 48, LANES), F32),
+            pltpu.VMEM((4, 2, 64, LANES), F32),
+            pltpu.VMEM((4, 2, 48, LANES), F32),
+            pltpu.VMEM((4, ROWS, LANES), F32),
+            pltpu.VMEM((2, 2, 2, ROWS, LANES), F32),
+            pltpu.VMEM((2, ROWS, LANES), F32),
+            pltpu.VMEM((2, 32, LANES), F32),
+            pltpu.VMEM((1, SLOTS), jnp.int32),
+            pltpu.SMEM((2, STRIPS), jnp.int32),
             pltpu.VMEM((COLUMNS, 8, LANES), jnp.int32),
             pltpu.VMEM((COLUMNS, LANES), jnp.int32),
             pltpu.VMEM((COLUMNS, LANES), jnp.int32),
@@ -551,19 +608,22 @@
             pltpu.VMEM((SLOTS, 2, 8, LANES), F32),
             pltpu.VMEM((COLUMNS * CAP, 2, 8, LANES), F32),
             dma((6, 2)),
-            dma((3, 4)),
-            dma((3, 4)),
+            dma((4, 4)),
+            dma((4, 4)),
             dma((COLUMNS,)),
             dma((COLUMNS,)),
             dma((COLUMNS,)),
             dma((COLUMNS,)),
-            dma,
+            dma((2,)),
         ],
         compiler_params=pltpu.CompilerParams(
-            collective_id=0, has_side_effects=True, vmem_limit_bytes=48 << 20
+            collective_id=0, has_side_effects=True, vmem_limit_bytes=20 << 20
         ),
         name="ocean",
-    )(tracers, face_speeds, ocean_block, ice_blocks.reshape(1, SLOTS))
+    )(*[
+        pltpu.with_memory_space_constraint(v, pltpu.HBM)
+        for v in (tracers, face_speeds, ocean_block.T, ice_blocks.reshape(1, SLOTS))
+    ])
     return pl.pallas_call(
         output_kernel,
         out_shape=(

time: 67.4 us -> 43.4 us (0.64)
  Pallas kernels: 62.5 us -> 42 us
  local copies, waits for them, and re-layouts: 3.63 us -> 0 us
    pallas_call x1, Pallas kernels: 59 us -> 38.4 us  [on_device(): pl.pallas_call(ocean_kernel, out_shape=(jax.ShapeDtypeStruct((2, LEVELS,...]
    unnamed x5 -> x0, local copies, waits for them, and re-layouts: 3.63 us -> none
where the time goes in v2:
time: 43.4 us; the launch traced here: 42.6 us
  Pallas kernels  42 us (97%)
  between operations  0.64 us (1%)
    pallas_call x1, Pallas kernels, on_device(): pl.pallas_call(ocean_kernel, out_shape=(jax.ShapeDtypeStruct((2, LEVELS,...  38.4 us
    pallas_call x1, Pallas kernels, on_device(): pl.pallas_call(output_kernel, out_shape=(jax.ShapeDtypeStruct(tracers.sha...  3.56 us

profile of v2, /device:TPU:39, one launch (start us, length us, event | category | flops | bytes accessed | tf_op | source)
XLA Modules:
  0.0 42.6 jit_solution(4312847560037236096)
XLA Ops:
  0.6 38.4 %ocean.1 = (f32[2,8,2,264,128]{4,3,2,1,0:T(8,128)S(1)}, f32[8,2,256,128]{3,2,1,0:T(8,128)S(1)}, f32[128,2,8,128]{3,2,1,0:T(8,128)S(1)}, s32[8,128]{1,0:T(8,128)S(1)}) custom-call(f32[2,8,256,256]{3,2,1,0:T(8,128)} %tracers.1, f32[2,2,8,256,256]{4,3,2,1,0:T(8,128)} %speeds.1, s32[2,32]{1,0:T(2,128)} %bitcast.2, s32[1,64]{1,0:T(1,128)} %bitcast.3), custom_call_target="tpu_custom_call" | custom-call | tf_op jit(solution)/shard_map/ocean/pallas_call | solution.py:582
  39.0 3.6 %outputs.1 = (f32[2,8,256,256]{3,2,1,0:T(8,128)}, f32[8,256,256]{2,1,0:T(8,128)}, f32[64,3,8,128]{3,2,1,0:T(8,128)}) custom-call(f32[2,8,2,264,128]{4,3,2,1,0:T(8,128)S(1)} %get-tuple-element.7.x, f32[8,2,256,128]{3,2,1,0:T(8,128)S(1)} %get-tuple-element.8.dens, f32[128,2,8,128]{3,2,1,0:T(8,128)S(1)} %get-tuple-element.9.incoming, ...), custom_call_target="tpu_custom_call" | custom-call | tf_op jit(solution)/shard_map/outputs/pallas_call | solution.py:627

commit v3 on v2

--- a/solution.py
+++ b/solution.py
@@ -158,48 +158,68 @@
     return index if isinstance(index, int) else pl.multiple_of(index, 8)
 
 
-def pack(x, speed, e, levels, cols, rows):
+def groups(body, count):
+    if count <= 3:
+        for g in range(8):
+            body(g, 0)
+    else:
+        lax.fori_loop(0, 8, body, 0, unroll=4)
+
+
+def pack_faces(speed, faces, levels, rows_list):
     lane = lax.broadcasted_iota(jnp.int32, (8, LANES), 1)
 
     def group(g, _):
         parts = []
         for q in range(4):
             here = pl.ds(aligned(g * 32 + q * 8), 8)
-            east = jnp.zeros((8, LANES), F32)
-            west = jnp.zeros((8, LANES), F32)
             face = jnp.zeros((8, LANES), F32)
             for k in levels:
-                for t in range(2):
-                    spot = 32 * q + 2 * (t * LEVELS + k)
-                    value = pltpu.roll(x[t, k, 1, here, :], spot + 1, 1)
-                    east = jnp.where(lane == spot, value, east)
-                    value = pltpu.roll(x[t, k, 0, here, :], spot + 1, 1)
-                    west = jnp.where(lane == spot + 1, value, west)
                 spot = 32 * q + 2 * k + 1
                 value = pltpu.roll(speed[0, k, 1, here, :], spot + 1, 1)
                 face = jnp.where(lane == spot, value, face)
-            parts.append((east, west, face))
-        east, west, face = [
-            (parts[0][i] + parts[1][i]) + (parts[2][i] + parts[3][i]) for i in range(3)
-        ]
+            parts.append(face)
+        face = (parts[0] + parts[1]) + (parts[2] + parts[3])
+        faces[pl.ds(aligned(g * 8), 8), :] = face + pltpu.roll(face, 2 * LEVELS, 1)
+        return 0
+
+    groups(group, len(levels))
+    for k in levels:
+        for half in range(2):
+            spot = 32 + k * 2 + half
+            for rows in rows_list:
+                rows[spot : spot + 1, :] = speed[1, k, half, ROWS - 1 : ROWS, :]
+
+
+def pack(x, faces, e, levels, cols, rows):
+    lane = lax.broadcasted_iota(jnp.int32, (8, LANES), 1)
+    pair = lane >> 1
+    odd = (lane & 1) != 0
+
+    def group(g, _):
+        parts = []
+        for q in range(4):
+            here = pl.ds(aligned(g * 32 + q * 8), 8)
+            both = jnp.zeros((8, LANES), F32)
+            for k in levels:
+                for t in range(2):
+                    spot = 16 * q + t * LEVELS + k
+                    ends = jnp.where(lane == 0, x[t, k, 0, here, :], x[t, k, 1, here, :])
+                    both = jnp.where(pair == spot, pltpu.roll(ends, 2 * spot + 1, 1), both)
+            parts.append(both)
+        both = (parts[0] + parts[1]) + (parts[2] + parts[3])
         here = pl.ds(aligned(g * 8), 8)
-        cols[e, 0, here, :] = (east + face) + pltpu.roll(face, 2 * LEVELS, 1)
-        cols[e, 1, here, :] = west
-        return 0
-
-    if len(levels) <= 3:
-        for g in range(8):
-            group(g, 0)
-    else:
-        lax.fori_loop(0, 8, group, 0, unroll=2)
+        cols[e, 0, here, :] = jnp.where(odd, faces[here, :], both)
+        cols[e, 1, here, :] = both
+        return 0
+
+    groups(group, len(levels))
     for k in levels:
         for half in range(2):
             for t in range(2):
                 spot = t * 16 + k * 2 + half
                 rows[e, 0, spot : spot + 1, :] = x[t, k, half, ROWS - 1 : ROWS, :]
                 rows[e, 1, spot : spot + 1, :] = x[t, k, half, 0:1, :]
-            spot = 32 + k * 2 + half
-            rows[e, 0, spot : spot + 1, :] = speed[1, k, half, ROWS - 1 : ROWS, :]
 
 
 def reversed_lanes(value):
@@ -302,7 +322,7 @@
 
 def ocean_kernel(
     tracers, speeds, land, own_list, x, dens, incoming, picks,
-    speed, cols, rows, cols_in, rows_in, edge, mix, ocean_v, flows, own_v, mask,
+    speed, cols, rows, cols_in, rows_in, edge, mix, ocean_v, flows, faces, own_v, mask,
     lists, stage, table, table_s, surf, outgoing,
     load_sem, send_sem, recv_sem, list_send, list_recv, relay_send, relay_recv, local_sem,
 ):
@@ -428,7 +448,8 @@
 
     for c in upper:
         c.wait()
-    pack(x, speed.at[0], 0, range(0, 3), cols, rows)
+    pack_faces(speed.at[0], faces.at[0], range(0, 3), [rows.at[0, 0]])
+    pack(x, faces.at[0], 0, range(0, 3), cols, rows)
     advance(x, speed.at[0], ocean_v, 0, 3)
     pl.semaphore_wait(barrier, COLUMNS - 1 + (1 - top) + inner)
     start_edges(0)
@@ -454,23 +475,23 @@
 
     for c in deep:
         c.wait()
-    pack(x, speed.at[0], 1, range(3, 8), cols, rows)
+    pack_faces(speed.at[0], faces.at[1], range(3, 8), [rows.at[1, 0]])
+    pack(x, faces.at[1], 1, range(3, 8), cols, rows)
     start_edges(1)
     advance(x, speed.at[0], ocean_v, 3, 8)
+    for c in late_low + late_high:
+        c.wait()
+    pack_faces(speed.at[1], faces.at[2], range(0, 8), [rows.at[2, 0], rows.at[3, 0]])
 
     fill(0, range(0, 3))
     settle(0, 0, 0, 2, False, None, None)
-    for c in late_low:
-        c.wait()
-    pack(x, speed.at[1], 2, range(0, 2), cols, rows)
+    pack(x, faces.at[2], 2, range(0, 2), cols, rows)
     start_edges(2)
     advance(x, speed.at[1], ocean_v, 0, 2)
 
     fill(1, range(3, 8))
     settle(1, 0, 2, 7, True, None, None)
-    for c in late_high:
-        c.wait()
-    pack(x, speed.at[1], 3, range(2, 8), cols, rows)
+    pack(x, faces.at[2], 3, range(2, 8), cols, rows)
     start_edges(3)
 
     def take_list(d, _):
@@ -482,7 +503,6 @@
     send_table(lists, gx, stage, table)
     fetch = pltpu.make_async_copy(table, table_s, local_sem.at[1])
     fetch.start()
-    pick_table(lists, gx, picks)
 
     fill(2, range(0, 2))
     settle(2, 1, 0, 1, False, dens, surf)
@@ -502,7 +522,7 @@
         )
 
     def relay_far(d, _):
-        peer = (1 - gx // 8) * 8 + lax.rem(gx + d, 8)
+        peer = (1 - gx // 8) * 8 + lax.rem(gx + d + 4, 8)
         bucket(peer, outgoing, peer * CAP)
         relay_copy(peer, gx).start()
         return 0
@@ -516,6 +536,7 @@
     lax.fori_loop(0, 8, relay_far, 0)
     lax.fori_loop(0, 7, relay_near, 0)
     bucket(gx, incoming, gx * CAP)
+    pick_table(lists, gx, picks)
 
     advance(x, speed.at[1], ocean_v, 2, 8)
     fill(3, range(2, 8))
@@ -599,6 +620,7 @@
             pltpu.VMEM((2, 2, 2, ROWS, LANES), F32),
             pltpu.VMEM((2, ROWS, LANES), F32),
             pltpu.VMEM((2, 32, LANES), F32),
+            pltpu.VMEM((3, 64, LANES), F32),
             pltpu.VMEM((1, SLOTS), jnp.int32),
             pltpu.SMEM((2, STRIPS), jnp.int32),
             pltpu.VMEM((COLUMNS, 8, LANES), jnp.int32),

time: 43.4 us -> 41 us (0.945); the launches traced: 42.6 us -> 40.9 us
  Pallas kernels: 42 us -> 40.2 us
    pallas_call x1, Pallas kernels: 38.4 us -> 36.7 us  [on_device(): pl.pallas_call(ocean_kernel, out_shape=(jax.ShapeDtypeStruct((2, LEVELS,...]
where the time goes in v3:
time: 41 us; the launch traced here: 40.9 us
  Pallas kernels  40.2 us (98%)
  between operations  0.64 us (2%)
    pallas_call x1, Pallas kernels, on_device(): pl.pallas_call(ocean_kernel, out_shape=(jax.ShapeDtypeStruct((2, LEVELS,...  36.7 us
    pallas_call x1, Pallas kernels, on_device(): pl.pallas_call(output_kernel, out_shape=(jax.ShapeDtypeStruct(tracers.sha...  3.56 us

profile of v3, /device:TPU:39, one launch (start us, length us, event | category | flops | bytes accessed | tf_op | source)
XLA Modules:
  0.0 40.9 jit_solution(8453425019393517889)
XLA Ops:
  0.6 36.7 %ocean.1 = (f32[2,8,2,264,128]{4,3,2,1,0:T(8,128)S(1)}, f32[8,2,256,128]{3,2,1,0:T(8,128)S(1)}, f32[128,2,8,128]{3,2,1,0:T(8,128)S(1)}, s32[8,128]{1,0:T(8,128)S(1)}) custom-call(f32[2,8,256,256]{3,2,1,0:T(8,128)} %tracers.1, f32[2,2,8,256,256]{4,3,2,1,0:T(8,128)} %speeds.1, s32[2,32]{1,0:T(2,128)} %bitcast.2, s32[1,64]{1,0:T(1,128)} %bitcast.3), custom_call_target="tpu_custom_call" | custom-call | tf_op jit(solution)/shard_map/ocean/pallas_call | solution.py:603
  37.3 3.6 %outputs.1 = (f32[2,8,256,256]{3,2,1,0:T(8,128)}, f32[8,256,256]{2,1,0:T(8,128)}, f32[64,3,8,128]{3,2,1,0:T(8,128)}) custom-call(f32[2,8,2,264,128]{4,3,2,1,0:T(8,128)S(1)} %get-tuple-element.7.x, f32[8,2,256,128]{3,2,1,0:T(8,128)S(1)} %get-tuple-element.8.dens, f32[128,2,8,128]{3,2,1,0:T(8,128)S(1)} %get-tuple-element.9.incoming, ...), custom_call_target="tpu_custom_call" | custom-call | tf_op jit(solution)/shard_map/outputs/pallas_call | solution.py:649

commit v4 on v3

--- a/solution.py
+++ b/solution.py
@@ -12,7 +12,7 @@
 ROWS = 256
 LANES = 128
 STRIPS = 32
-CHUNK = 64
+RELAY = ((1, 4), (1, 5), (0, 4), (1, 6), (1, 7), (0, 5), (1, 0), (1, 1), (0, 3), (1, 2), (1, 3), (0, 6), (0, 2), (0, 7), (0, 1))
 COLUMNS = 16
 TOP = 7
 CAP = 8
@@ -82,12 +82,12 @@
     lax.fori_loop(low, high, level, 0)
 
 
-def settle_levels(x, edge, mix, ocean_v, first, last, resumed, dens, surf):
-    lane = lax.broadcasted_iota(jnp.int32, (CHUNK, LANES), 1)
+def settle_levels(x, edge, mix, ocean_v, first, last, resumed, dens, surf, size):
+    lane = lax.broadcasted_iota(jnp.int32, (size, LANES), 1)
     first_lane, last_lane = lane == 0, lane == LANES - 1
 
     def chunk(c, _):
-        here = pl.ds(pl.multiple_of(c * CHUNK, CHUNK), CHUNK)
+        here = pl.ds(aligned(c * size), size)
         rim = edge[here, :]
         ocean = [ocean_v[half, here, :] for half in range(2)]
 
@@ -117,8 +117,8 @@
                     x[t, k, half, here, :] = value
                     done.append(value)
                     if surf is not None and k == 0:
-                        for i in range(CHUNK // 8):
-                            tile = 2 * (c * (CHUNK // 8) + i) + half
+                        for i in range(size // 8):
+                            tile = 2 * (c * (size // 8) + i) + half
                             surf[tile, t] = value[8 * i : 8 * i + 8]
                 if dens is not None:
                     dens[k, half, here, :] = density_at(done[0], done[1], k)
@@ -151,7 +151,10 @@
                     mix[t, half, here, :] = over[t][half]
         return 0
 
-    lax.fori_loop(0, ROWS // CHUNK, chunk, 0)
+    if size == ROWS:
+        chunk(0, 0)
+    else:
+        lax.fori_loop(0, ROWS // size, chunk, 0)
 
 
 def aligned(index):
@@ -159,7 +162,7 @@
 
 
 def groups(body, count):
-    if count <= 3:
+    if count <= 6:
         for g in range(8):
             body(g, 0)
     else:
@@ -334,23 +337,6 @@
     north_row = gy + 1 - top
     north_col = gx + top * (COLUMNS - 1 - 2 * gx)
 
-    barrier = pltpu.get_barrier_semaphore()
-
-    def greet(d, _):
-        peer = lax.rem(gx + 1 + d, COLUMNS)
-        pl.semaphore_signal(barrier, inc=1, device_id=(gy, peer), device_id_type=MESH)
-        return 0
-
-    lax.fori_loop(0, COLUMNS - 1, greet, 0)
-
-    @pl.when(gy < TOP)
-    def _():
-        pl.semaphore_signal(barrier, inc=1, device_id=(gy + 1, gx), device_id_type=MESH)
-
-    @pl.when(gy > 0)
-    def _():
-        pl.semaphore_signal(barrier, inc=1, device_id=(gy - 1, gx), device_id_type=MESH)
-
     def load_x(i, lo, hi):
         return [
             pltpu.make_async_copy(
@@ -379,7 +365,27 @@
     deep = load_x(2, 3, 8) + load_speed(3, 0, 3, 8)
     late_low = load_speed(4, 1, 0, 2)
     late_high = load_speed(5, 1, 2, 8)
-    for c in upper + deep + late_low + late_high:
+    for c in upper:
+        c.start()
+
+    barrier = pltpu.get_barrier_semaphore()
+
+    def greet(d, _):
+        peer = lax.rem(gx + 1 + d, COLUMNS)
+        pl.semaphore_signal(barrier, inc=1, device_id=(gy, peer), device_id_type=MESH)
+        return 0
+
+    lax.fori_loop(0, COLUMNS - 1, greet, 0)
+
+    @pl.when(gy < TOP)
+    def _():
+        pl.semaphore_signal(barrier, inc=1, device_id=(gy + 1, gx), device_id_type=MESH)
+
+    @pl.when(gy > 0)
+    def _():
+        pl.semaphore_signal(barrier, inc=1, device_id=(gy - 1, gx), device_id_type=MESH)
+
+    for c in deep + late_low + late_high:
         c.start()
 
     blocks.wait()
@@ -470,8 +476,10 @@
         wait_edges(e)
         unpack(x, e, levels, cols, rows, cols_in, rows_in, edge, ocean_v, flows, top, gy > 0)
 
-    def settle(e, m, first, last, resumed, dens_ref, surf_ref):
-        settle_levels(x, edge.at[e], mix.at[m], ocean_v, first, last, resumed, dens_ref, surf_ref)
+    def settle(e, m, first, last, resumed, dens_ref, surf_ref, size):
+        settle_levels(
+            x, edge.at[e], mix.at[m], ocean_v, first, last, resumed, dens_ref, surf_ref, size
+        )
 
     for c in deep:
         c.wait()
@@ -484,28 +492,28 @@
     pack_faces(speed.at[1], faces.at[2], range(0, 8), [rows.at[2, 0], rows.at[3, 0]])
 
     fill(0, range(0, 3))
-    settle(0, 0, 0, 2, False, None, None)
+    settle(0, 0, 0, 2, False, None, None, 256)
     pack(x, faces.at[2], 2, range(0, 2), cols, rows)
     start_edges(2)
     advance(x, speed.at[1], ocean_v, 0, 2)
 
-    fill(1, range(3, 8))
-    settle(1, 0, 2, 7, True, None, None)
-    pack(x, faces.at[2], 3, range(2, 8), cols, rows)
-    start_edges(3)
-
     def take_list(d, _):
         peer = lax.rem(gx + 1 + d, COLUMNS)
         list_copy(peer, peer).wait_recv()
         return 0
 
     lax.fori_loop(0, COLUMNS - 1, take_list, 0)
+    fill(1, range(3, 8))
+    settle(1, 0, 2, 7, True, None, None, 128)
     send_table(lists, gx, stage, table)
+    pack(x, faces.at[2], 3, range(2, 8), cols, rows)
     fetch = pltpu.make_async_copy(table, table_s, local_sem.at[1])
     fetch.start()
+    start_edges(3)
+
 
     fill(2, range(0, 2))
-    settle(2, 1, 0, 1, False, dens, surf)
+    settle(2, 1, 0, 1, False, dens, surf, 256)
     fetch.wait()
 
     def bucket(peer, target, base):
@@ -521,26 +529,20 @@
             device_id=(gy, peer), device_id_type=MESH,
         )
 
-    def relay_far(d, _):
-        peer = (1 - gx // 8) * 8 + lax.rem(gx + d + 4, 8)
+    def relay(side, turn):
+        peer = side * 8 + lax.rem(gx + turn, 8)
         bucket(peer, outgoing, peer * CAP)
         relay_copy(peer, gx).start()
-        return 0
-
-    def relay_near(d, _):
-        peer = (gx // 8) * 8 + lax.rem(gx + 1 + d, 8)
-        bucket(peer, outgoing, peer * CAP)
-        relay_copy(peer, gx).start()
-        return 0
-
-    lax.fori_loop(0, 8, relay_far, 0)
-    lax.fori_loop(0, 7, relay_near, 0)
+
+    side = gx // 8
+    for across, turn in RELAY:
+        relay(1 - side if across else side, turn)
     bucket(gx, incoming, gx * CAP)
     pick_table(lists, gx, picks)
 
     advance(x, speed.at[1], ocean_v, 2, 8)
     fill(3, range(2, 8))
-    settle(3, 1, 1, 7, True, dens, None)
+    settle(3, 1, 1, 7, True, dens, None, 128)
 
     for e in range(4):
         finish_edges(e)
@@ -555,8 +557,10 @@
     lax.fori_loop(0, COLUMNS - 1, close, 0)
 
 
-def output_kernel(x, dens, incoming, picks, tracers_out, dens_out, ice_out, ice, sems):
+def output_kernel(x, dens, incoming, picks_v, tracers_out, dens_out, ice_out, ice, picks, sems):
     copies = []
+    table = pltpu.make_async_copy(picks_v, picks, sems.at[6])
+    table.start()
     for half in range(2):
         lanes = pl.ds(half * LANES, LANES)
         copies.append(
@@ -571,6 +575,7 @@
         )
     for c in copies:
         c.start()
+    table.wait()
 
     def slot(s, _):
         place = picks[0, s]
@@ -597,7 +602,6 @@
 def on_device(tracers, face_speeds, ocean_block, ice_blocks):
     anywhere = pl.BlockSpec(memory_space=pl.ANY)
     vmem = pl.BlockSpec(memory_space=pltpu.VMEM)
-    smem = pl.BlockSpec(memory_space=pltpu.SMEM)
     hbm = pl.BlockSpec(memory_space=pltpu.HBM)
     dma = pltpu.SemaphoreType.DMA
     x, dens, incoming, picks = pl.pallas_call(
@@ -653,9 +657,13 @@
             jax.ShapeDtypeStruct(tracers.shape[1:], F32),
             jax.ShapeDtypeStruct((SLOTS, 3, 8, LANES), F32),
         ),
-        in_specs=[anywhere, anywhere, vmem, smem],
+        in_specs=[anywhere, anywhere, vmem, vmem],
         out_specs=(anywhere, anywhere, anywhere),
-        scratch_shapes=[pltpu.VMEM((SLOTS, 3, 8, LANES), F32), dma((6,))],
+        scratch_shapes=[
+            pltpu.VMEM((SLOTS, 3, 8, LANES), F32),
+            pltpu.SMEM((8, LANES), jnp.int32),
+            dma((7,)),
+        ],
         compiler_params=pltpu.CompilerParams(vmem_limit_bytes=16 << 20),
         name="outputs",
     )(x, dens, incoming, picks)

time: 41 us -> 38 us (0.927)
  Pallas kernels: 40.2 us -> 37.2 us
    pallas_call x1, Pallas kernels: 36.7 us -> 34.3 us  [on_device(): pl.pallas_call(ocean_kernel, out_shape=(jax.ShapeDtypeStruct((2, LEVELS,...]
    pallas_call x1, Pallas kernels: 3.56 us -> 2.97 us  [on_device(): pl.pallas_call(output_kernel, out_shape=(jax.ShapeDtypeStruct(tracers.sha...]
where the time goes in v4:
time: 38 us; the launch traced here: 37.9 us
  Pallas kernels  37.2 us (98%)
  between operations  0.64 us (2%)
    pallas_call x1, Pallas kernels, on_device(): pl.pallas_call(ocean_kernel, out_shape=(jax.ShapeDtypeStruct((2, LEVELS,...  34.3 us
    pallas_call x1, Pallas kernels, on_device(): pl.pallas_call(output_kernel, out_shape=(jax.ShapeDtypeStruct(tracers.sha...  2.97 us

profile of v4, /device:TPU:39, one launch (start us, length us, event | category | flops | bytes accessed | tf_op | source)
XLA Modules:
  0.0 37.9 jit_solution(18016813235459787712)
XLA Ops:
  0.6 34.3 %ocean.1 = (f32[2,8,2,264,128]{4,3,2,1,0:T(8,128)S(1)}, f32[8,2,256,128]{3,2,1,0:T(8,128)S(1)}, f32[128,2,8,128]{3,2,1,0:T(8,128)S(1)}, s32[8,128]{1,0:T(8,128)S(1)}) custom-call(f32[2,8,256,256]{3,2,1,0:T(8,128)} %tracers.1, f32[2,2,8,256,256]{4,3,2,1,0:T(8,128)} %speeds.1, s32[2,32]{1,0:T(2,128)} %bitcast.2, s32[1,64]{1,0:T(1,128)} %bitcast.3), custom_call_target="tpu_custom_call" | custom-call | tf_op jit(solution)/shard_map/ocean/pallas_call | solution.py:607
  34.9 3.0 %outputs.1 = (f32[2,8,256,256]{3,2,1,0:T(8,128)}, f32[8,256,256]{2,1,0:T(8,128)}, f32[64,3,8,128]{3,2,1,0:T(8,128)}) custom-call(f32[2,8,2,264,128]{4,3,2,1,0:T(8,128)S(1)} %get-tuple-element.7.x, f32[8,2,256,128]{3,2,1,0:T(8,128)S(1)} %get-tuple-element.8.dens, f32[128,2,8,128]{3,2,1,0:T(8,128)S(1)} %get-tuple-element.9.incoming, ...), custom_call_target="tpu_custom_call" | custom-call | tf_op jit(solution)/shard_map/outputs/pallas_call | solution.py:653

commit v5 on v4

--- a/solution.py
+++ b/solution.py
@@ -122,6 +122,10 @@
                             surf[tile, t] = value[8 * i : 8 * i + 8]
                 if dens is not None:
                     dens[k, half, here, :] = density_at(done[0], done[1], k)
+
+        if dens is not None:
+            for half in range(2):
+                dens[0, half, here, :] = density_at(x[0, 0, half, here, :], x[1, 0, half, here, :], 0)
 
         over = None
         if resumed:
@@ -513,7 +517,7 @@
 
 
     fill(2, range(0, 2))
-    settle(2, 1, 0, 1, False, dens, surf, 256)
+    settle(2, 1, 0, 1, False, None, surf, 256)
     fetch.wait()
 
     def bucket(peer, target, base):
@@ -540,21 +544,23 @@
     bucket(gx, incoming, gx * CAP)
     pick_table(lists, gx, picks)
 
+    def close_list(d, _):
+        list_copy(lax.rem(gx + 1 + d, COLUMNS), gx).wait_send()
+        return 0
+
+    lax.fori_loop(0, COLUMNS - 1, close_list, 0)
     advance(x, speed.at[1], ocean_v, 2, 8)
     fill(3, range(2, 8))
     settle(3, 1, 1, 7, True, dens, None, 128)
-
     for e in range(4):
         finish_edges(e)
 
-    def close(d, _):
-        peer = lax.rem(gx + 1 + d, COLUMNS)
-        list_copy(peer, gx).wait_send()
+    for across, turn in RELAY:
+        peer = (1 - side if across else side) * 8 + lax.rem(gx + turn, 8)
         relay_copy(peer, gx).wait_send()
+    for across, turn in RELAY:
+        peer = (1 - side if across else side) * 8 + lax.rem(gx + 8 - turn, 8)
         relay_copy(peer, peer).wait_recv()
-        return 0
-
-    lax.fori_loop(0, COLUMNS - 1, close, 0)
 
 
 def output_kernel(x, dens, incoming, picks_v, tracers_out, dens_out, ice_out, ice, picks, sems):

time: 38 us -> 37.8 us (level)
  no operation moved by 1% of the time
where the time goes in v5:
time: 37.8 us; the launch traced here: 37.7 us
  Pallas kernels  37.1 us (98%)
  between operations  0.64 us (2%)
    pallas_call x1, Pallas kernels, on_device(): pl.pallas_call(ocean_kernel, out_shape=(jax.ShapeDtypeStruct((2, LEVELS,...  34.1 us
    pallas_call x1, Pallas kernels, on_device(): pl.pallas_call(output_kernel, out_shape=(jax.ShapeDtypeStruct(tracers.sha...  2.97 us

profile of v5, /device:TPU:39, one launch (start us, length us, event | category | flops | bytes accessed | tf_op | source)
XLA Modules:
  0.0 37.7 jit_solution(11633623761554106441)
XLA Ops:
  0.6 34.1 %ocean.1 = (f32[2,8,2,264,128]{4,3,2,1,0:T(8,128)S(1)}, f32[8,2,256,128]{3,2,1,0:T(8,128)S(1)}, f32[128,2,8,128]{3,2,1,0:T(8,128)S(1)}, s32[8,128]{1,0:T(8,128)S(1)}) custom-call(f32[2,8,256,256]{3,2,1,0:T(8,128)} %tracers.1, f32[2,2,8,256,256]{4,3,2,1,0:T(8,128)} %speeds.1, s32[2,32]{1,0:T(2,128)} %bitcast.2, s32[1,64]{1,0:T(1,128)} %bitcast.3), custom_call_target="tpu_custom_call" | custom-call | tf_op jit(solution)/shard_map/ocean/pallas_call | solution.py:613
  34.7 3.0 %outputs.1 = (f32[2,8,256,256]{3,2,1,0:T(8,128)}, f32[8,256,256]{2,1,0:T(8,128)}, f32[64,3,8,128]{3,2,1,0:T(8,128)}) custom-call(f32[2,8,2,264,128]{4,3,2,1,0:T(8,128)S(1)} %get-tuple-element.7.x, f32[8,2,256,128]{3,2,1,0:T(8,128)S(1)} %get-tuple-element.8.dens, f32[128,2,8,128]{3,2,1,0:T(8,128)S(1)} %get-tuple-element.9.incoming, ...), custom_call_target="tpu_custom_call" | custom-call | tf_op jit(solution)/shard_map/outputs/pallas_call | solution.py:659
